TPU v7x, 32 devices: a whole 2x2x4 slice. The times are simulated.
32 devices in a mesh: dp: 4 (over y, core), fsdp: 8 (over z, x).
Axes of the slice: x: 2, y: 2, z: 4, core: 2. Of those that a mesh axis runs over, the one named last changes fastest.
Arguments:
- features: bfloat16 [1536, 49, 2048], P(('dp', 'fsdp')), may hold values from -15 to 15
- view_order: int32 [32, 48], P(('dp', 'fsdp')), may hold values from 0 to 47, each once within a row
- conv_one: float32 [2048, 512], P('fsdp', 'dp'), may hold values from -0.125 to 0.125
- conv_two: float32 [4608, 512], P('fsdp', 'dp'), may hold values from -0.09375 to 0.09375
- conv_three: float32 [512, 2048], P('fsdp', 'dp'), may hold values from -0.25 to 0.25
- proj_one: float32 [2048, 1024], P('fsdp', 'dp'), may hold values from -0.125 to 0.125
- proj_two: float32 [1024, 128], P('fsdp', 'dp'), may hold values from -0.1875 to 0.1875
- norm_params: float32 [2, 4096], P(None, ('dp', 'fsdp')), may hold values from -2 to 3, as said below
- first_conv_one: float32 [2048, 512], P('fsdp', 'dp'), may hold values from -6.1035156e-05 to 6.1035156e-05
- first_conv_two: float32 [4608, 512], P('fsdp', 'dp'), may hold values from -6.1035156e-05 to 6.1035156e-05
- first_conv_three: float32 [512, 2048], P('fsdp', 'dp'), may hold values from -6.1035156e-05 to 6.1035156e-05
- first_proj_one: float32 [2048, 1024], P('fsdp', 'dp'), may hold values from -6.1035156e-05 to 6.1035156e-05
- first_proj_two: float32 [1024, 128], P('fsdp', 'dp'), may hold values from -6.1035156e-05 to 6.1035156e-05
- first_norm: float32 [2, 4096], P(None, ('dp', 'fsdp')), may hold values from -6.1035156e-05 to 6.1035156e-05
- second_conv_one: float32 [2048, 512], P('fsdp', 'dp'), may hold values from 7.4706436e-13 to 1.195303e-11
- second_conv_two: float32 [4608, 512], P('fsdp', 'dp'), may hold values from 7.4706436e-13 to 1.195303e-11
- second_conv_three: float32 [512, 2048], P('fsdp', 'dp'), may hold values from 7.4706436e-13 to 1.195303e-11
- second_proj_one: float32 [2048, 1024], P('fsdp', 'dp'), may hold values from 7.4706436e-13 to 1.195303e-11
- second_proj_two: float32 [1024, 128], P('fsdp', 'dp'), may hold values from 7.4706436e-13 to 1.195303e-11
- second_norm: float32 [2, 4096], P(None, ('dp', 'fsdp')), may hold values from 7.4706436e-13 to 1.195303e-11
Outputs:
- loss: float32 [], replicated
- input_grad: float32 [1536, 49, 2048], P(('dp', 'fsdp'))
- grad_norm: float32 [], replicated
- new_conv_one: float32 [2048, 512], P('fsdp', 'dp')
- new_conv_two: float32 [4608, 512], P('fsdp', 'dp')
- new_conv_three: float32 [512, 2048], P('fsdp', 'dp')
- new_proj_one: float32 [2048, 1024], P('fsdp', 'dp')
- new_proj_two: float32 [1024, 128], P('fsdp', 'dp')
- new_norm: float32 [2, 4096], P(None, ('dp', 'fsdp'))
- new_first_conv_one: float32 [2048, 512], P('fsdp', 'dp')
- new_first_conv_two: float32 [4608, 512], P('fsdp', 'dp')
- new_first_conv_three: float32 [512, 2048], P('fsdp', 'dp')
- new_first_proj_one: float32 [2048, 1024], P('fsdp', 'dp')
- new_first_proj_two: float32 [1024, 128], P('fsdp', 'dp')
- new_first_norm: float32 [2, 4096], P(None, ('dp', 'fsdp'))
- new_second_conv_one: float32 [2048, 512], P('fsdp', 'dp')
- new_second_conv_two: float32 [4608, 512], P('fsdp', 'dp')
- new_second_conv_three: float32 [512, 2048], P('fsdp', 'dp')
- new_second_proj_one: float32 [2048, 1024], P('fsdp', 'dp')
- new_second_proj_two: float32 [1024, 128], P('fsdp', 'dp')
- new_second_norm: float32 [2, 4096], P(None, ('dp', 'fsdp'))
Inputs may be any that keep to these rules, and one draw needn't show every extreme that they name: `view_order`: in row d, entry j = 2 i + k says that slot j of that device's views holds view k of image d * 24 + i. `norm_params`: row 0 is positive.
All inputs are finite; a program needn't handle non-finite values.
Results may differ from a plain program's by a relative error of at most 0.039.
Values may be sent and summed in bfloat16 or wider, within the bound.
A program may use at most 384 MiB of HBM per device.

v0:
```python
import jax
import jax.numpy as jnp
from jax import lax
from jax.sharding import PartitionSpec as P

C_IN = 2048
C_MID = 512
P_HID = 1024
P_OUT = 128
SIDE = 7
STEP = 10
PIX = 49


highest = lax.Precision.HIGHEST
norm_epsilon = 1e-05
ridge_term = 0.01
clip_level = 0.1
beta_first = 0.9
beta_second = 0.999
adam_epsilon = 1e-08
decay_rate = 0.05
norm_rate = 0.5


def gelu_exact(values):
    return jax.nn.gelu(values, approximate=False)


def gelu_back(values, upstream):
    return jax.vjp(gelu_exact, values)[1](upstream)[0]


def matmul(left, right):
    return jnp.dot(left, right, preferred_element_type=jnp.float32)


def contract_rows(left, right):
    return lax.dot_general(
        left, right, (((0,), (0,)), ((), ())), preferred_element_type=jnp.float32
    )


def contract_cols(left, right):
    return lax.dot_general(
        left, right, (((1,), (1,)), ((), ())), preferred_element_type=jnp.float32
    )


def gather_weights(weight_one, weight_two, weight_three, weight_four, weight_five, norm_low):
    outer = (
        lax.all_gather(weight_one, "fsdp", axis=0, tiled=True),
        lax.all_gather(weight_two, "fsdp", axis=0, tiled=True),
        lax.all_gather(weight_three, "fsdp", axis=0, tiled=True),
        lax.all_gather(weight_four, "fsdp", axis=0, tiled=True),
        lax.all_gather(weight_five, "fsdp", axis=0, tiled=True),
        lax.all_gather(norm_low, "fsdp", axis=1, tiled=True),
    )
    return (
        lax.all_gather(outer[0], "dp", axis=1, tiled=True),
        lax.all_gather(outer[1], "dp", axis=1, tiled=True),
        lax.all_gather(outer[2], "dp", axis=1, tiled=True),
        lax.all_gather(outer[3], "dp", axis=1, tiled=True),
        lax.all_gather(outer[4], "dp", axis=1, tiled=True),
        lax.all_gather(outer[5], "dp", axis=1, tiled=True),
    )


def gather_again(weight_one, weight_two, weight_three, weight_four, weight_five, norm_low):
    outer = (
        lax.all_gather(weight_one, "fsdp", axis=0, tiled=True),
        lax.all_gather(weight_two, "fsdp", axis=0, tiled=True),
        lax.all_gather(weight_three, "fsdp", axis=0, tiled=True),
        lax.all_gather(weight_four, "fsdp", axis=0, tiled=True),
        lax.all_gather(weight_five, "fsdp", axis=0, tiled=True),
        lax.all_gather(norm_low, "fsdp", axis=1, tiled=True),
    )
    return (
        lax.all_gather(outer[0], "dp", axis=1, tiled=True),
        lax.all_gather(outer[1], "dp", axis=1, tiled=True),
        lax.all_gather(outer[2], "dp", axis=1, tiled=True),
        lax.all_gather(outer[3], "dp", axis=1, tiled=True),
        lax.all_gather(outer[4], "dp", axis=1, tiled=True),
        lax.all_gather(outer[5], "dp", axis=1, tiled=True),
    )


def reduce_inner(grad_one, grad_two, grad_three, grad_four, grad_five):
    return (
        lax.psum_scatter(grad_one, "dp", scatter_dimension=1, tiled=True),
        lax.psum_scatter(grad_two, "dp", scatter_dimension=1, tiled=True),
        lax.psum_scatter(grad_three, "dp", scatter_dimension=1, tiled=True),
        lax.psum_scatter(grad_four, "dp", scatter_dimension=1, tiled=True),
        lax.psum_scatter(grad_five, "dp", scatter_dimension=1, tiled=True),
    )


def reduce_outer(grad_one, grad_two, grad_three, grad_four, grad_five):
    return (
        lax.psum_scatter(grad_one, "fsdp", scatter_dimension=0, tiled=True),
        lax.psum_scatter(grad_two, "fsdp", scatter_dimension=0, tiled=True),
        lax.psum_scatter(grad_three, "fsdp", scatter_dimension=0, tiled=True),
        lax.psum_scatter(grad_four, "fsdp", scatter_dimension=0, tiled=True),
        lax.psum_scatter(grad_five, "fsdp", scatter_dimension=0, tiled=True),
    )


def norm_forward(hidden, gain_part, shift_part, count_all):
    moment_sums = lax.psum(
        (jnp.sum(hidden, axis=0), jnp.sum(hidden * hidden, axis=0)), ("dp", "fsdp")
    )
    mean_value = moment_sums[0] / count_all
    scaling = lax.rsqrt(moment_sums[1] / count_all - mean_value * mean_value + norm_epsilon)
    normed = (hidden - mean_value) * scaling
    return (normed * gain_part + shift_part, normed, scaling)


def norm_backward(upstream, normed, scaling, gain_part, count_all):
    grad_sums = lax.psum(
        (jnp.sum(upstream, axis=0), jnp.sum(upstream * normed, axis=0)), ("dp", "fsdp")
    )
    shift_grad = grad_sums[0]
    gain_grad = grad_sums[1]
    hidden_grad = (
        gain_part * scaling * (upstream - shift_grad / count_all - normed * gain_grad / count_all)
    )
    return (hidden_grad, gain_grad, shift_grad)


def spread_columns(activation, view_count):
    picture = activation.reshape(view_count, SIDE, SIDE, C_MID)
    padded = jnp.pad(picture, ((0, 0), (1, 1), (1, 1), (0, 0)))
    pieces = [
        padded[:, vertical : vertical + SIDE, lateral : lateral + SIDE, :]
        for vertical in range(3)
        for lateral in range(3)
    ]
    return jnp.stack(pieces, axis=3).reshape(-1, 9 * C_MID)


def fold_columns(columns_grad, view_count):
    picture = columns_grad.reshape(view_count, SIDE, SIDE, 9, C_MID)
    summed = jnp.zeros((view_count, SIDE, SIDE, C_MID), jnp.float32)
    for vertical in range(3):
        for lateral in range(3):
            placed = jnp.pad(
                picture[:, :, :, 3 * vertical + lateral, :],
                ((0, 0), (vertical, 2 - vertical), (lateral, 2 - lateral), (0, 0)),
            )
            summed = summed + placed[:, 1 : 1 + SIDE, 1 : 1 + SIDE, :]
    return summed.reshape(-1, C_MID)


def local_objective(sorted_embed, mean_embed, covariance):
    unit_views = []
    for view_index in range(2):
        factor = jnp.linalg.cholesky(covariance[view_index])
        whitened = lax.linalg.triangular_solve(
            factor,
            (sorted_embed[:, view_index] - mean_embed[view_index]).T,
            left_side=True,
            lower=True,
        )
        unit_views.append(
            whitened * lax.rsqrt(jnp.mean(whitened * whitened, axis=0) + norm_epsilon)
        )
    return jnp.sum(jnp.mean((unit_views[0] - unit_views[1]) ** 2, axis=0))


def adam_update(weight, moment_one, moment_two, gradient, step_rate, weight_decay):
    first_new = beta_first * moment_one + (1.0 - beta_first) * gradient
    second_new = beta_second * moment_two + (1.0 - beta_second) * gradient * gradient
    first_hat = first_new / (1.0 - beta_first**STEP)
    second_hat = second_new / (1.0 - beta_second**STEP)
    weight_new = weight - step_rate * (
        first_hat / (jnp.sqrt(second_hat) + adam_epsilon) + weight_decay * weight
    )
    return (weight_new, first_new, second_new)


def body(
    features,
    view_order,
    conv_one,
    conv_two,
    conv_three,
    proj_one,
    proj_two,
    norm_params,
    first_conv_one,
    first_conv_two,
    first_conv_three,
    first_proj_one,
    first_proj_two,
    first_norm,
    second_conv_one,
    second_conv_two,
    second_conv_three,
    second_proj_one,
    second_proj_two,
    second_norm,
):
    devices = lax.axis_size("dp") * lax.axis_size("fsdp")
    view_count = features.shape[0]
    row_total = view_count * PIX * devices
    view_total = view_count * devices
    image_total = view_total // 2
    start_two = C_MID
    start_three = 2 * C_MID
    start_four = 2 * C_MID + C_IN
    low_one = conv_one.astype(jnp.bfloat16)
    low_two = conv_two.astype(jnp.bfloat16)
    low_three = conv_three.astype(jnp.bfloat16)
    low_four = proj_one.astype(jnp.bfloat16)
    low_five = proj_two.astype(jnp.bfloat16)
    low_norm = norm_params.astype(jnp.bfloat16)
    gathered = gather_weights(low_one, low_two, low_three, low_four, low_five, low_norm)
    norm_full = gathered[5].astype(jnp.float32)
    gain_all = norm_full[0]
    shift_all = norm_full[1]
    gain_one = gain_all[:start_two]
    gain_two = gain_all[start_two:start_three]
    gain_three = gain_all[start_three:start_four]
    gain_four = gain_all[start_four:]
    pixel_rows = features.reshape(-1, C_IN)
    hidden_one = matmul(pixel_rows, gathered[0])
    out_one, normed_one, scale_one = norm_forward(
        hidden_one, gain_one, shift_all[:start_two], row_total
    )
    act_one = gelu_exact(out_one).astype(jnp.bfloat16)
    columns = spread_columns(act_one, view_count)
    hidden_two = matmul(columns, gathered[1])
    out_two, normed_two, scale_two = norm_forward(
        hidden_two, gain_two, shift_all[start_two:start_three], row_total
    )
    act_two = gelu_exact(out_two).astype(jnp.bfloat16)
    hidden_three = matmul(act_two, gathered[2])
    out_three, normed_three, scale_three = norm_forward(
        hidden_three, gain_three, shift_all[start_three:start_four], row_total
    )
    summed = out_three + pixel_rows.astype(jnp.float32)
    block_out = gelu_exact(summed)
    pooled = jnp.mean(block_out.reshape(view_count, PIX, C_IN), axis=1).astype(jnp.bfloat16)
    proj_hidden = matmul(pooled, gathered[3])
    out_four, normed_four, scale_four = norm_forward(
        proj_hidden, gain_four, shift_all[start_four:], view_total
    )
    proj_act = gelu_exact(out_four).astype(jnp.bfloat16)
    embedding = matmul(proj_act, gathered[4])
    selector = (view_order[0][:, None] == jnp.arange(view_count, dtype=jnp.int32)[None, :]).astype(
        jnp.float32
    )
    sorted_flat = lax.dot_general(selector, embedding, (((0,), (0,)), ((), ())), precision=highest)
    sorted_embed = sorted_flat.reshape(view_count // 2, 2, P_OUT)
    view_sums = jnp.sum(sorted_embed, axis=0)
    view_outer = jnp.einsum("ikp,ikq->kpq", sorted_embed, sorted_embed, precision=highest)
    view_sums, view_outer = lax.psum((view_sums, view_outer), ("dp", "fsdp"))
    mean_embed = view_sums / image_total
    covariance = (
        view_outer / image_total
        - mean_embed[:, :, None] * mean_embed[:, None, :]
        + ridge_term * jnp.eye(P_OUT, dtype=jnp.float32)[None]
    )
    local_total, pullback = jax.vjp(local_objective, sorted_embed, mean_embed, covariance)
    direct, mean_grad, cov_grad = pullback(jnp.ones((), jnp.float32))
    mean_grad, cov_grad, objective = lax.psum((mean_grad, cov_grad, local_total), ("dp", "fsdp"))
    symmetric = cov_grad + jnp.swapaxes(cov_grad, 1, 2)
    correction = mean_grad - jnp.einsum("kpq,kq->kp", symmetric, mean_embed, precision=highest)
    sorted_grad = (
        direct
        + (
            jnp.einsum("ikp,kpq->ikq", sorted_embed, symmetric, precision=highest)
            + correction[None]
        )
        / image_total
    )
    embed_grad = jnp.dot(
        selector, sorted_grad.reshape(view_count, P_OUT), precision=highest
    ).astype(jnp.bfloat16)
    back_weights = gather_again(low_one, low_two, low_three, low_four, low_five, low_norm)
    grad_five = contract_rows(proj_act, embed_grad)
    act_four_grad = contract_cols(embed_grad, back_weights[4])
    four_grad, gain_four_grad, shift_four_grad = norm_backward(
        gelu_back(out_four, act_four_grad), normed_four, scale_four, gain_four, view_total
    )
    four_low = four_grad.astype(jnp.bfloat16)
    grad_four = contract_rows(pooled, four_low)
    pooled_grad = contract_cols(four_low, back_weights[3])
    block_grad = jnp.broadcast_to((pooled_grad / PIX)[:, None, :], (view_count, PIX, C_IN)).reshape(
        -1, C_IN
    )
    summed_grad = gelu_back(summed, block_grad)
    three_grad, gain_three_grad, shift_three_grad = norm_backward(
        summed_grad, normed_three, scale_three, gain_three, row_total
    )
    three_low = three_grad.astype(jnp.bfloat16)
    grad_three = contract_rows(act_two, three_low)
    act_two_grad = contract_cols(three_low, back_weights[2])
    two_grad, gain_two_grad, shift_two_grad = norm_backward(
        gelu_back(out_two, act_two_grad), normed_two, scale_two, gain_two, row_total
    )
    two_low = two_grad.astype(jnp.bfloat16)
    grad_two = contract_rows(columns, two_low)
    act_one_grad = fold_columns(contract_cols(two_low, back_weights[1]), view_count)
    one_grad, gain_one_grad, shift_one_grad = norm_backward(
        gelu_back(out_one, act_one_grad), normed_one, scale_one, gain_one, row_total
    )
    one_low = one_grad.astype(jnp.bfloat16)
    grad_one = contract_rows(pixel_rows, one_low)
    input_grad = (summed_grad + contract_cols(one_low, back_weights[0])).reshape(
        view_count, PIX, C_IN
    )
    partial_value = reduce_inner(grad_one, grad_two, grad_three, grad_four, grad_five)
    owned = reduce_outer(
        partial_value[0], partial_value[1], partial_value[2], partial_value[3], partial_value[4]
    )
    norm_grad_full = jnp.stack(
        [
            jnp.concatenate([gain_one_grad, gain_two_grad, gain_three_grad, gain_four_grad]),
            jnp.concatenate([shift_one_grad, shift_two_grad, shift_three_grad, shift_four_grad]),
        ]
    )
    shard_width = norm_params.shape[1]
    owner_index = lax.axis_index(("dp", "fsdp"))
    norm_owned = lax.dynamic_slice_in_dim(norm_grad_full, owner_index * shard_width, shard_width, 1)
    param_grads = (owned[0], owned[1], owned[2], owned[3], owned[4], norm_owned)
    local_squares = jnp.float32(0.0)
    for member in param_grads:
        local_squares = local_squares + jnp.sum(member * member)
    squares = lax.psum(local_squares, ("dp", "fsdp"))
    grad_norm = jnp.sqrt(squares)
    factor = clip_level / jnp.maximum(grad_norm, clip_level)
    masters = (conv_one, conv_two, conv_three, proj_one, proj_two, norm_params)
    firsts = (
        first_conv_one,
        first_conv_two,
        first_conv_three,
        first_proj_one,
        first_proj_two,
        first_norm,
    )
    seconds = (
        second_conv_one,
        second_conv_two,
        second_conv_three,
        second_proj_one,
        second_proj_two,
        second_norm,
    )
    step_rates = (
        C_IN ** (-0.5),
        (9 * C_MID) ** (-0.5),
        C_MID ** (-0.5),
        C_IN ** (-0.5),
        P_HID ** (-0.5),
        norm_rate,
    )
    decays = (decay_rate, decay_rate, decay_rate, decay_rate, decay_rate, 0.0)
    results = [
        adam_update(
            masters[place],
            firsts[place],
            seconds[place],
            param_grads[place] * factor,
            step_rates[place],
            decays[place],
        )
        for place in range(6)
    ]
    return (
        objective / image_total,
        input_grad,
        grad_norm,
        results[0][0],
        results[1][0],
        results[2][0],
        results[3][0],
        results[4][0],
        results[5][0],
        results[0][1],
        results[1][1],
        results[2][1],
        results[3][1],
        results[4][1],
        results[5][1],
        results[0][2],
        results[1][2],
        results[2][2],
        results[3][2],
        results[4][2],
        results[5][2],
    )


def solution(mesh):
    placed = (
        P(("dp", "fsdp"), None, None),
        P(("dp", "fsdp"), None),
        P("fsdp", "dp"),
        P("fsdp", "dp"),
        P("fsdp", "dp"),
        P("fsdp", "dp"),
        P("fsdp", "dp"),
        P(None, ("dp", "fsdp")),
        P("fsdp", "dp"),
        P("fsdp", "dp"),
        P("fsdp", "dp"),
        P("fsdp", "dp"),
        P("fsdp", "dp"),
        P(None, ("dp", "fsdp")),
        P("fsdp", "dp"),
        P("fsdp", "dp"),
        P("fsdp", "dp"),
        P("fsdp", "dp"),
        P("fsdp", "dp"),
        P(None, ("dp", "fsdp")),
    )
    return jax.shard_map(
        body,
        mesh=mesh,
        in_specs=placed,
        out_specs=(
            P(),
            P(("dp", "fsdp"), None, None),
            P(),
            P("fsdp", "dp"),
            P("fsdp", "dp"),
            P("fsdp", "dp"),
            P("fsdp", "dp"),
            P("fsdp", "dp"),
            P(None, ("dp", "fsdp")),
            P("fsdp", "dp"),
            P("fsdp", "dp"),
            P("fsdp", "dp"),
            P("fsdp", "dp"),
            P("fsdp", "dp"),
            P(None, ("dp", "fsdp")),
            P("fsdp", "dp"),
            P("fsdp", "dp"),
            P("fsdp", "dp"),
            P("fsdp", "dp"),
            P("fsdp", "dp"),
            P(None, ("dp", "fsdp")),
        ),
        check_vma=False,
    )
```

profile of v0, /device:TPU:0, one launch (start us, length us, event | category | flops | bytes accessed | tf_op | source)
XLA Modules:
  0.0 2051.8 jit_solution(2928805482470155851)
XLA Ops:
  11.6 35.7 %all_gather.46 = bf16[2048,128]{1,0:T(8,128)(2,1)} all-gather(bf16[256,128]{1,0:T(8,128)(2,1)S(1)} %convert_element_type.77), channel_id=1, replica_groups=mesh['dp'=4,'fsdp'=8] {'fsdp'}, dimensions={0}, use_global_device_ids=true | all-gather | bytes 589824 | tf_op jit(solution)/shard_map/all_gather | solution.py:52
  57.3 34.1 %all_gather.52 = bf16[512,512]{1,0:T(8,128)(2,1)} all-gather(bf16[64,512]{1,0:T(8,128)(2,1)S(1)} %convert_element_type.83), channel_id=1, replica_groups=mesh['dp'=4,'fsdp'=8] {'fsdp'}, dimensions={0}, use_global_device_ids=true | all-gather | bytes 589824 | tf_op jit(solution)/shard_map/all_gather | solution.py:54
  136.8 26.0 %all_gather.56 = bf16[1024,32]{0,1:T(8,128)(2,1)S(1)} all-gather(bf16[128,32]{0,1:T(8,128)(2,1)S(1)} %convert_element_type.88), channel_id=1, replica_groups=mesh['dp'=4,'fsdp'=8] {'fsdp'}, dimensions={0}, use_global_device_ids=true | all-gather | bytes 73728 | tf_op jit(solution)/shard_map/all_gather | solution.py:56
  179.2 38.1 %all-reduce.23 = (f32[512]{0:T(512)S(1)}, f32[512]{0:T(512)S(1)}) all-reduce(f32[512]{0:T(512)S(1)} %get-tuple-element.294, f32[512]{0:T(512)S(1)} %get-tuple-element.293), channel_id=1, replica_groups=mesh['dp'=4,'fsdp'=8] {'dp','fsdp'}, use_global_device_ids=true, to_apply=%region_3.0 | all-reduce | flops 1024 | bytes 8192 | tf_op jit(solution)/shard_map/psum | solution.py:109
  259.0 22.4 %copy.523 = bf16[48,7,7,9,512]{4,3,2,1,0:T(8,128)(2,1)} copy(bf16[48,7,7,9,512]{4,2,1,0,3:T(8,128)(2,1)} %fusion.41) | data formatting | bytes 43352064 | tf_op jit(solution)/shard_map/stack | solution.py:138
  281.4 28.2 %copy.622 = bf16[294,8,9,512]{3,1,2,0:T(8,128)(2,1)} copy(bf16[294,8,9,512]{3,2,1,0:T(8,128)(2,1)} %bitcast.247) | data formatting | bytes 43352064
  309.6 18.5 fusion.139
  328.1 41.4 %all-reduce.22 = (f32[512]{0:T(512)S(1)}, f32[512]{0:T(512)S(1)}) all-reduce(f32[512]{0:T(512)S(1)} %get-tuple-element.292, f32[512]{0:T(512)S(1)} %get-tuple-element.291), channel_id=1, replica_groups=mesh['dp'=4,'fsdp'=8] {'dp','fsdp'}, use_global_device_ids=true, to_apply=%region_7.8 | all-reduce | flops 1024 | bytes 8192 | tf_op jit(solution)/shard_map/psum | solution.py:109
  394.7 39.1 %all-reduce.21 = (f32[2048]{0:T(1024)S(1)}, f32[2048]{0:T(1024)S(1)}) all-reduce(f32[2048]{0:T(1024)S(1)} %get-tuple-element.286, f32[2048]{0:T(1024)S(1)} %get-tuple-element.285), channel_id=1, replica_groups=mesh['dp'=4,'fsdp'=8] {'dp','fsdp'}, use_global_device_ids=true, to_apply=%region_11.12 | all-reduce | flops 4096 | bytes 32768 | tf_op jit(solution)/shard_map/psum | solution.py:109
  433.8 47.7 %multiply_multiply_fusion.5 = (f32[2352,2048]{1,0:T(8,128)}, f32[2352,2048]{1,0:T(8,128)}) fusion(bf16[2352,2048]{1,0:T(8,128)(2,1)} %reshape.185, f32[2048]{0:T(1024)S(1)} %bitcast.277, f32[2048]{0:T(1024)S(1)} %bitcast.275, f32[2048]{0:T(1024)S(1)} %get-tuple-element.372, f32[2352,2048]{1,0:T(8,128)} %get-tuple-element.397, f32[2048]{0:T(1024)S(1)} %get-tuple-element.381), kind=kLoop, calls=%fused_computation.21 | loop fusion | flops 337182720 | bytes 67469312 | tf_op jit(solution)/shard_map/mul | solution.py:27
  508.4 41.5 %all-reduce.20 = (f32[1024]{0:T(1024)S(1)}, f32[1024]{0:T(1024)S(1)}) all-reduce(f32[1024]{0:T(1024)S(1)} %get-tuple-element.298, f32[1024]{0:T(1024)S(1)} %get-tuple-element.297), channel_id=1, replica_groups=mesh['dp'=4,'fsdp'=8] {'dp','fsdp'}, use_global_device_ids=true, to_apply=%region_16.17 | all-reduce | flops 2048 | bytes 16384 | tf_op jit(solution)/shard_map/psum | solution.py:109
  551.9 38.6 %psum.163 = f32[2,128]{1,0:T(2,128)S(1)} all-reduce(f32[2,128]{1,0:T(2,128)S(1)} %reduce_sum.313), channel_id=1, replica_groups=mesh['dp'=4,'fsdp'=8] {'dp','fsdp'}, use_global_device_ids=true, to_apply=%region_19.20 | all-reduce | flops 256 | bytes 2048 | tf_op jit(solution)/shard_map/psum | solution.py:257
  590.8 122.8 %all-reduce.27.cloned.1.call-done = f32[2,128,128]{1,2,0:T(8,128)} async-done(((f32[2,128,128]{1,2,0:T(8,128)}), f32[2,128,128]{1,2,0:T(8,128)}) %all-reduce.27.cloned.1.call-update) | async-done | bytes 131088 | tf_op jit(solution)/shard_map/psum | solution.py:257
  787.4 39.3 %psum.166 = f32[2,128]{1,0:T(2,128)S(1)} all-reduce(f32[2,128]{1,0:T(2,128)S(1)} %pad_add_fusion.1), channel_id=1, replica_groups=mesh['dp'=4,'fsdp'=8] {'dp','fsdp'}, use_global_device_ids=true, to_apply=%region_32.37 | all-reduce | flops 256 | bytes 2048 | tf_op jit(solution)/shard_map/psum | solution.py:266
  826.7 82.4 %all-reduce.29.cloned.1.call-done = f32[2,128,128]{2,1,0:T(8,128)} async-done(((f32[2,128,128]{2,1,0:T(8,128)}), f32[2,128,128]{2,1,0:T(8,128)}) %all-reduce.29.cloned.1.call-update) | async-done | bytes 131088 | tf_op jit(solution)/shard_map/psum | solution.py:266
  914.0 39.3 %all-reduce.19 = (f32[1024]{0:T(1024)S(1)}, f32[1024]{0:T(1024)S(1)}) all-reduce(f32[1024]{0:T(1024)S(1)} %get-tuple-element.296, f32[1024]{0:T(1024)S(1)} %get-tuple-element.295), channel_id=1, replica_groups=mesh['dp'=4,'fsdp'=8] {'dp','fsdp'}, use_global_device_ids=true, to_apply=%region_36.41 | all-reduce | flops 2048 | bytes 16384 | tf_op jit(solution)/shard_map/psum | solution.py:119
  983.3 30.7 %fusion.135 = (f32[2048]{0:T(1024)S(1)}, f32[2048]{0:T(1024)S(1)}, f32[2352,2048]{1,0:T(8,128)}) fusion(f32[2048]{0:T(1024)S(1)} %get-tuple-element.372, f32[2352,2048]{1,0:T(8,128)} %get-tuple-element.397, f32[2048]{0:T(1024)S(1)} %get-tuple-element.381, f32[2352,2048]{1,0:T(8,128)} %reshape.191, f32[2352,2048]{1,0:T(8,128)} %get-tuple-element.349, ...), kind=kLoop, calls=%fused_computation.321 | loop fusion | flops 105967616 | bytes 86753280 | tf_op jit(solution)/shard_map/reduce_sum | solution.py:120
  1014.0 40.1 %all-reduce.18 = (f32[2048]{0:T(1024)S(1)}, f32[2048]{0:T(1024)S(1)}) all-reduce(f32[2048]{0:T(1024)S(1)} %get-tuple-element.284, f32[2048]{0:T(1024)S(1)} %get-tuple-element.283), channel_id=1, replica_groups=mesh['dp'=4,'fsdp'=8] {'dp','fsdp'}, use_global_device_ids=true, to_apply=%region_40.45 | all-reduce | flops 4096 | bytes 32768 | tf_op jit(solution)/shard_map/psum | solution.py:119
  1083.2 40.2 %all-reduce.17 = (f32[512]{0:T(512)S(1)}, f32[512]{0:T(512)S(1)}) all-reduce(f32[512]{0:T(512)S(1)} %get-tuple-element.290, f32[512]{0:T(512)S(1)} %get-tuple-element.289), channel_id=1, replica_groups=mesh['dp'=4,'fsdp'=8] {'dp','fsdp'}, use_global_device_ids=true, to_apply=%region_44.49 | all-reduce | flops 1024 | bytes 8192 | tf_op jit(solution)/shard_map/psum | solution.py:119
  1130.6 20.4 fusion.163
  1151.0 52.2 %reshape.192 = f32[48,7,7,9,512]{4,3,2,1,0:T(8,128)} reshape(f32[2352,4608]{1,0:T(8,128)} %fusion.163) | data formatting | bytes 86704128 | tf_op jit(solution)/shard_map/reshape | solution.py:142
  1213.0 123.9 %fusion.155 = (f32[48,7,7,1,512]{4,3,2,1,0:T(1,128)}, f32[48,7,7,1,512]{4,3,2,1,0:T(1,128)}, f32[48,7,7,1,512]{4,3,2,1,0:T(1,128)}, f32[48,7,7,1,512]{4,3,2,1,0:...) fusion(f32[48,7,7,9,512]{4,3,2,1,0:T(8,128)} %reshape.192), kind=kLoop, calls=%fused_computation.329 | loop fusion | bytes 86704128 | tf_op jit(solution)/shard_map/slice | solution.py:147
  1391.8 39.9 %all-reduce.16 = (f32[512]{0:T(512)S(1)}, f32[512]{0:T(512)S(1)}) all-reduce(f32[512]{0:T(512)S(1)} %get-tuple-element.288, f32[512]{0:T(512)S(1)} %get-tuple-element.287), channel_id=1, replica_groups=mesh['dp'=4,'fsdp'=8] {'dp','fsdp'}, use_global_device_ids=true, to_apply=%region_48.53 | all-reduce | flops 1024 | bytes 8192 | tf_op jit(solution)/shard_map/psum | solution.py:119
  1451.2 21.5 %fusion.164 = f32[4608,512]{1,0:T(8,128)} fusion(bf16[2352,4608]{1,0:T(8,128)(2,1)} %bitcast.249, bf16[2352,512]{1,0:T(8,128)(2,1)} %copy-done.8), kind=kOutput, calls=%fused_computation.338 | convolution fusion | flops 11098128384 | bytes 33521664 | tf_op jit(solution)/shard_map/dot_general | solution.py:39
  1491.2 74.3 %reduce-scatter.23.cloned.1.call-done = f32[2048,256]{1,0:T(8,128)} async-done(((f32[2048,1024]{1,0:T(8,128)}), f32[2048,256]{1,0:T(8,128)}) %reduce-scatter.23.cloned.1.call-update) | async-done | bytes 2097168 | tf_op jit(solution)/shard_map/reduce_scatter | solution.py:93
  1565.5 81.6 %reduce-scatter.15.cloned.1.call-done = f32[4608,128]{1,0:T(8,128)} async-done(((f32[4608,512]{1,0:T(8,128)}), f32[4608,128]{1,0:T(8,128)}) %reduce-scatter.15.cloned.1.call-update) | async-done | bytes 2359312 | tf_op jit(solution)/shard_map/reduce_scatter | solution.py:91
  1676.8 20.6 %copy.565 = f32[48,49,2048]{2,0,1:T(8,128)} copy(f32[48,49,2048]{2,1,0:T(8,128)} %reshape.194) | data formatting | bytes 38535168
  1712.9 64.5 %reduce-scatter.21.cloned.1.call-done = f32[64,512]{1,0:T(8,128)} async-done(((f32[512,512]{1,0:T(8,128)}), f32[64,512]{1,0:T(8,128)}) %reduce-scatter.21.cloned.1.call-update) | async-done | bytes 131088 | tf_op jit(solution)/shard_map/reduce_scatter | solution.py:102
  1778.9 65.1 %reduce-scatter.13.cloned.1.call-done = f32[256,128]{0,1:T(8,128)} async-done(((f32[2048,128]{0,1:T(8,128)}), f32[256,128]{0,1:T(8,128)}) %reduce-scatter.13.cloned.1.call-update) | async-done | bytes 131088 | tf_op jit(solution)/shard_map/reduce_scatter | solution.py:100
  1845.6 68.6 %reduce-scatter.25.cloned.1.call-done = f32[256,256]{1,0:T(8,128)} async-done(((f32[2048,256]{1,0:T(8,128)}), f32[256,256]{1,0:T(8,128)}) %reduce-scatter.25.cloned.1.call-update) | async-done | bytes 262160 | tf_op jit(solution)/shard_map/reduce_scatter | solution.py:103
  1915.9 69.8 %reduce-scatter.17.cloned.1.call-done = f32[576,128]{1,0:T(8,128)} async-done(((f32[4608,128]{1,0:T(8,128)}), f32[576,128]{1,0:T(8,128)}) %reduce-scatter.17.cloned.1.call-update) | async-done | bytes 294928 | tf_op jit(solution)/shard_map/reduce_scatter | solution.py:101
  1991.3 39.8 %all-reduce.15 = (f32[]{:T(128)}, f32[]{:T(128)}) all-reduce(f32[]{:T(128)} %get-tuple-element.408, f32[]{:T(128)S(6)} %add.398), channel_id=1, replica_groups=mesh['dp'=4,'fsdp'=8] {'dp','fsdp'}, use_global_device_ids=true, to_apply=%region_26.0 | all-reduce | flops 2 | bytes 16 | tf_op jit(solution)/shard_map/psum | solution.py:266
  (346 shorter events, 480.1 us)
Async XLA Ops:
  7.2 49.1 %all-gather.9.cloned.1.call-start = ((), (), s32[]{:S(2)}) async-start(), calls=%async_computation.11 | async-start | bytes 1327104 | tf_op jit(solution)/shard_map/all_gather | solution.py:53
  8.9 159.8 %all-gather.15.cloned.1.call-start = ((), (), s32[]{:S(2)}) async-start(), calls=%async_computation.14 | async-start | bytes 1179648 | tf_op jit(solution)/shard_map/all_gather | solution.py:55
  10.6 158.2 %all-gather.7.cloned.1.call-start = ((), (), s32[]{:S(2)}) async-start(), calls=%async_computation.10 | async-start | bytes 2621440 | tf_op jit(solution)/shard_map/all_gather | solution.py:60
  47.3 262.2 %all-gather.11.cloned.1.call-start = ((), (), s32[]{:S(2)}) async-start(), calls=%async_computation.12 | async-start | bytes 5898240 | tf_op jit(solution)/shard_map/all_gather | solution.py:61
  56.3 326.2 %all-gather.13.cloned.1.call-start = ((), (), s32[]{:S(2)}) async-start(), calls=%async_computation.13 | async-start | bytes 2621440 | tf_op jit(solution)/shard_map/all_gather | solution.py:62
  91.4 413.8 %all-gather.17.cloned.1.call-start = ((), (), s32[]{:S(2)}) async-start(), calls=%async_computation.15 | async-start | bytes 5242880 | tf_op jit(solution)/shard_map/all_gather | solution.py:63
  168.7 544.9 %all-reduce.27.cloned.1.call-start = ((), (), s32[]{:S(2)}) async-start(), calls=%async_computation.16 | async-start | bytes 262144 | tf_op jit(solution)/shard_map/psum | solution.py:257
  590.5 318.5 %all-reduce.29.cloned.1.call-start = ((), (), s32[]{:S(2)}) async-start(), calls=%async_computation.17 | async-start | bytes 262144 | tf_op jit(solution)/shard_map/psum | solution.py:266
  787.4 685.4 %reduce-scatter.27.cloned.1.call-start = ((), (), s32[]{:S(2)}) async-start(), calls=%async_computation.26 | async-start | bytes 655360 | tf_op jit(solution)/shard_map/reduce_scatter | solution.py:94
  953.3 520.0 %reduce-scatter.19.cloned.1.call-start = ((), (), s32[]{:S(2)}) async-start(), calls=%async_computation.22 | async-start | bytes 5242880 | tf_op jit(solution)/shard_map/reduce_scatter | solution.py:92
  1212.8 278.4 %reduce-scatter.11.cloned.1.call-start = ((), (), s32[]{:S(2)}) async-start(), calls=%async_computation.18 | async-start | bytes 5242880 | tf_op jit(solution)/shard_map/reduce_scatter | solution.py:90
  1446.5 119.0 %reduce-scatter.23.cloned.1.call-start = ((), (), s32[]{:S(2)}) async-start(), calls=%async_computation.24 | async-start | bytes 10485760 | tf_op jit(solution)/shard_map/reduce_scatter | solution.py:93
  1451.1 196.0 %reduce-scatter.15.cloned.1.call-start = ((), (), s32[]{:S(2)}) async-start(), calls=%async_computation.20 | async-start | bytes 11796480 | tf_op jit(solution)/shard_map/reduce_scatter | solution.py:91
  1472.7 238.8 %reduce-scatter.29.cloned.1.call-start = ((), (), s32[]{:S(2)}) async-start(), calls=%async_computation.27 | async-start | bytes 147456 | tf_op jit(solution)/shard_map/reduce_scatter | solution.py:104
  1473.3 304.1 %reduce-scatter.21.cloned.1.call-start = ((), (), s32[]{:S(2)}) async-start(), calls=%async_computation.23 | async-start | bytes 1179648 | tf_op jit(solution)/shard_map/reduce_scatter | solution.py:102
  1473.9 370.2 %reduce-scatter.13.cloned.1.call-start = ((), (), s32[]{:S(2)}) async-start(), calls=%async_computation.19 | async-start | bytes 1179648 | tf_op jit(solution)/shard_map/reduce_scatter | solution.py:100
  1491.2 423.1 %reduce-scatter.25.cloned.1.call-start = ((), (), s32[]{:S(2)}) async-start(), calls=%async_computation.25 | async-start | bytes 2359296 | tf_op jit(solution)/shard_map/reduce_scatter | solution.py:103
  1565.5 420.2 %reduce-scatter.17.cloned.1.call-start = ((), (), s32[]{:S(2)}) async-start(), calls=%async_computation.21 | async-start | bytes 2654208 | tf_op jit(solution)/shard_map/reduce_scatter | solution.py:101
  1676.7 359.1 %copy-start.51 = (f32[2,128]{1,0:T(2,128)S(1)}, f32[2,128]{1,0:T(2,128)}, u32[]{:S(2)}) copy-start(f32[2,128]{1,0:T(2,128)} %param.39) | copy-start | bytes 3076
  1676.7 359.1 %copy-start.52 = (f32[2,128]{1,0:T(2,128)S(1)}, f32[2,128]{1,0:T(2,128)}, u32[]{:S(2)}) copy-start(f32[2,128]{1,0:T(2,128)} %param.45) | copy-start | bytes 3076
  1676.7 359.1 %copy-start.53 = (f32[2,128]{1,0:T(2,128)S(1)}, f32[2,128]{1,0:T(2,128)}, u32[]{:S(2)}) copy-start(f32[2,128]{1,0:T(2,128)} %param.51) | copy-start | bytes 3076
  1676.7 359.7 %copy-start.25 = (f32[128,32]{0,1:T(8,128)S(1)}, f32[128,32]{0,1:T(8,128)}, u32[]{:S(2)}) copy-start(f32[128,32]{0,1:T(8,128)} %param.38) | copy-start | bytes 49156
  1676.7 359.6 %copy-start.41 = (f32[128,32]{0,1:T(8,128)S(1)}, f32[128,32]{0,1:T(8,128)}, u32[]{:S(2)}) copy-start(f32[128,32]{0,1:T(8,128)} %param.44) | copy-start | bytes 49156
  1676.7 359.6 %copy-start.42 = (f32[128,32]{0,1:T(8,128)S(1)}, f32[128,32]{0,1:T(8,128)}, u32[]{:S(2)}) copy-start(f32[128,32]{0,1:T(8,128)} %param.50) | copy-start | bytes 49156
  1676.7 361.0 %copy-start.14 = (f32[64,512]{1,0:T(8,128)S(1)}, f32[64,512]{1,0:T(8,128)}, u32[]{:S(2)}) copy-start(f32[64,512]{1,0:T(8,128)} %param.36) | copy-start | bytes 393220
  1676.7 361.0 %copy-start.20 = (f32[64,512]{1,0:T(8,128)S(1)}, f32[64,512]{1,0:T(8,128)}, u32[]{:S(2)}) copy-start(f32[64,512]{1,0:T(8,128)} %param.42) | copy-start | bytes 393220
  1676.8 361.0 %copy-start.21 = (f32[64,512]{1,0:T(8,128)S(1)}, f32[64,512]{1,0:T(8,128)}, u32[]{:S(2)}) copy-start(f32[64,512]{1,0:T(8,128)} %param.48) | copy-start | bytes 393220
  1676.8 362.7 %copy-start.11 = (f32[256,256]{1,0:T(8,128)S(1)}, f32[256,256]{1,0:T(8,128)}, u32[]{:S(2)}) copy-start(f32[256,256]{1,0:T(8,128)} %param.37) | copy-start | bytes 786436
  1676.8 362.7 %copy-start.18 = (f32[256,256]{1,0:T(8,128)S(1)}, f32[256,256]{1,0:T(8,128)}, u32[]{:S(2)}) copy-start(f32[256,256]{1,0:T(8,128)} %param.43) | copy-start | bytes 786436
  1676.8 362.6 %copy-start.19 = (f32[256,256]{1,0:T(8,128)S(1)}, f32[256,256]{1,0:T(8,128)}, u32[]{:S(2)}) copy-start(f32[256,256]{1,0:T(8,128)} %param.49) | copy-start | bytes 786436
  1697.4 344.0 %copy-start.9 = (f32[576,128]{1,0:T(8,128)S(1)}, f32[576,128]{1,0:T(8,128)}, u32[]{:S(2)}) copy-start(f32[576,128]{1,0:T(8,128)} %param.35) | copy-start | bytes 884740
  1697.5 343.9 %copy-start.16 = (f32[576,128]{1,0:T(8,128)S(1)}, f32[576,128]{1,0:T(8,128)}, u32[]{:S(2)}) copy-start(f32[576,128]{1,0:T(8,128)} %param.41) | copy-start | bytes 884740
  (54 other events, 2281.3 us)
Sparse Core Ops, SparseCore 0:
  10.8 45.4 all-gather.8
  59.0 40.4 all-gather.14
  101.1 21.6 all-gather.6
  124.1 38.1 all-gather.10
  163.7 22.9 all-gather.12
  188.1 35.9 all-gather.16
  590.7 122.9 all-reduce.26
  787.5 121.5 all-reduce.28
  953.5 21.5 reduce-scatter.26
  1212.9 44.3 reduce-scatter.18
  1446.6 44.4 reduce-scatter.10
  1493.7 71.6 reduce-scatter.22
  1568.6 78.4 reduce-scatter.14
  1650.3 61.2 reduce-scatter.28
  1714.8 62.5 reduce-scatter.20
  1781.0 62.9 reduce-scatter.12
  1847.4 66.7 reduce-scatter.24
  1917.6 68.0 reduce-scatter.16
where the time goes:
time: 2060 us; the launch traced here: 2050 us
  waiting for transfers between devices  670 us (33%)
  blocking collectives  561 us (27%)
  local copies, waits for them, and re-layouts  397 us (19%)
  other arithmetic  246 us (12%)
  matrix products  152 us (7%)
  between operations  23.2 us (1%)
    psum x4, blocking collectives, norm_forward(): lax.psum((jnp.sum(hidden, axis=0), jnp.sum(hidden * hidden, axis=0)), ('d...  160 us
    psum x4, blocking collectives, norm_backward(): lax.psum((jnp.sum(upstream, axis=0), jnp.sum(upstream * normed, axis=0)),...  160 us
    slice x9, local copies, waits for them, and re-layouts, fold_columns(): picture[:, :, :, 3 * vertical + lateral, :]  146 us
    psum x1, waiting for transfers between devices, body(): view_sums, view_outer = lax.psum((view_sums, view_outer), ('dp', 'fsdp'))  123 us
    unnamed x153, local copies, waits for them, and re-layouts  86 us
    psum x1, waiting for transfers between devices, body(): lax.psum((mean_grad, cov_grad, local_total), ('dp', 'fsdp'))  82.4 us
    reduce_scatter x1, waiting for transfers between devices, reduce_inner(): lax.psum_scatter(grad_two, 'dp', scatter_dimension=1, tiled=True)  81.6 us
    psum x2, blocking collectives, body(): lax.psum((mean_grad, cov_grad, local_total), ('dp', 'fsdp'))  79 us
  transfers between devices with their start and end apart: 18, of which 11 were waited for; matrix products, arithmetic and copies ran while one was open for 34% of the time, Pallas kernels for 0%

commit v1 on v0

v1 whole, which is shorter than its diff:
```python
from typing import Any, NamedTuple

import jax
import jax.numpy as jnp
from jax import lax
from jax.experimental import pallas as pl
from jax.experimental.pallas import tpu as pltpu
from jax.sharding import PartitionSpec as P

C_IN = 2048
C_MID = 512
P_HID = 1024
P_OUT = 128
SIDE = 7
STEP = 10
PIX = 49
LANES = 128
BLOCKS = C_IN // C_MID
CHUNKS = SIDE


highest = lax.Precision.HIGHEST
bf16 = jnp.bfloat16
f32 = jnp.float32
norm_epsilon = 1e-05
ridge_term = 0.01
clip_level = 0.1
beta_first = 0.9
beta_second = 0.999
adam_epsilon = 1e-08
decay_rate = 0.05
norm_rate = 0.5
bell_scale = 0.3989422804014327
root_half = 0.5**0.5
bell_rate = -0.7213475204444817
DP, FSDP = "dp", "fsdp"


def gelu_pair(values):
    below = 0.5 + 0.5 * lax.erf(values * root_half)
    bell = jnp.exp2(values * values * bell_rate)
    return values * below, below + values * bell * bell_scale


def dot(left, right):
    return jnp.dot(left, right, preferred_element_type=f32)


def dot_cols(left, right):
    return lax.dot_general(left, right, (((1,), (1,)), ((), ())), preferred_element_type=f32)


def dot_rows(left, right):
    return lax.dot_general(left, right, (((0,), (0,)), ((), ())), preferred_element_type=f32)


def exact_cols(left, right):
    return lax.dot_general(
        left, right, (((1,), (1,)), ((), ())), precision=highest, preferred_element_type=f32
    )


def exact_rows(left, right):
    return lax.dot_general(
        left, right, (((0,), (0,)), ((), ())), precision=highest, preferred_element_type=f32
    )


def exact_dot(left, right):
    return jnp.dot(left, right, precision=highest, preferred_element_type=f32)


def inverse_factors(matrices):
    row_top = lax.broadcasted_iota(jnp.int32, (8, P_OUT), 0)
    row_all = lax.broadcasted_iota(jnp.int32, (P_OUT, P_OUT), 0)
    col_all = lax.broadcasted_iota(jnp.int32, (P_OUT, P_OUT), 1)

    def one_step(place, left, right):
        scale = lax.rsqrt(left[place : place + 1, place : place + 1])
        left_row = left[place : place + 1, :] * scale
        right_row = right[place : place + 1, :] * scale
        column = left[:, place : place + 1] * scale
        left = left - column * left_row
        right = right - column * right_row
        here = row_top == place
        left = jnp.concatenate([jnp.where(here, 0.0, left[:8]), left[8:]], axis=0)
        right = jnp.concatenate(
            [jnp.where(here, jnp.broadcast_to(right_row, (8, P_OUT)), right[:8]), right[8:]], axis=0
        )
        return left, right

    def panel(_, pairs):
        pairs = list(pairs)
        for place in range(8):
            for which in range(len(pairs)):
                pairs[which] = one_step(place, *pairs[which])
        return tuple(
            (
                pltpu.roll(jnp.concatenate([left[8:], left[:8]], axis=0), P_OUT - 8, 1),
                jnp.concatenate([right[8:], right[:8]], axis=0),
            )
            for left, right in pairs
        )

    start = tuple((matrix, (row_all == col_all).astype(f32)) for matrix in matrices)
    done = lax.fori_loop(0, P_OUT // 8, panel, start)
    return [right for _, right in done]


def pack_pair(first, second):
    row = lax.broadcasted_iota(jnp.int32, (P_OUT, P_OUT), 0)
    col = lax.broadcasted_iota(jnp.int32, (P_OUT, P_OUT), 1)
    packed = jnp.where(row >= col, first, second.T)
    diagonal = jnp.sum(jnp.where(row == col, second, 0.0), axis=0, keepdims=True)
    return packed, diagonal


def unpack_pair(packed, diagonal):
    row = lax.broadcasted_iota(jnp.int32, (P_OUT, P_OUT), 0)
    col = lax.broadcasted_iota(jnp.int32, (P_OUT, P_OUT), 1)
    turned = packed.T
    first = jnp.where(row >= col, packed, turned)
    second = jnp.where(row < col, packed, jnp.where(row == col, diagonal, turned))
    return first, second


class Ins(NamedTuple):
    features: Any
    order: Any
    norm: Any
    shards: Any


class Outs(NamedTuple):
    slope: Any
    one_low: Any
    low_one: Any
    pool_grad: Any
    norm_grad: Any
    scalars: Any
    grads: Any


class SumRoom(NamedTuple):
    dp: Any
    fsdp: Any
    s0: Any
    r0: Any
    s1: Any
    r1: Any


class MatrixRoom(NamedTuple):
    pack: Any
    dp: Any
    fsdp: Any
    all: Any
    s0: Any
    r0: Any
    s1: Any
    r1: Any
    s2: Any
    r2: Any


class Mem(NamedTuple):
    w: Any
    r3: Any
    r4: Any
    r5: Any
    stage: Any
    stage_sem: Any
    column_sem: Any
    h1: Any
    d1: Any
    h2: Any
    d2: Any
    a2: Any
    h3: Any
    pad1: Any
    pad2: Any
    pool: Any
    pool_slope: Any
    pool_bend: Any
    pooled: Any
    proj_act: Any
    proj_slope: Any
    proj_hidden: Any
    coef: Any
    stats: Any
    norm: Any
    norm_tiles: Any
    norm_s0: Any
    norm_r0: Any
    norm_s1: Any
    norm_r1: Any
    bulk_send: Any
    bulk_recv: Any
    mats: Any
    sums: Any
    squares: Any


class Plan:
    def __init__(self, dp_size, fsdp_size, views, inside):
        self.dp = dp_size
        self.fsdp = fsdp_size
        self.devices = dp_size * fsdp_size
        self.views = views
        self.rows = views * PIX
        self.chunk = views * SIDE
        self.inside = inside
        self.z = 4
        self.x = 2
        self.half = (128, 288, 32, 128, 16)
        self.width = (128, 128, 512, 256, 128)
        piece = P_OUT + 8
        self.embed_rows = -(-piece // (8 * dp_size)) * 8


def kernel(plan, *refs):
    ins, outs, mem = Ins(*refs[:3], refs[3:8]), Outs(*refs[8:14], refs[14:19]), refs[19]
    views, chunk, rows = plan.views, plan.chunk, plan.rows
    row_total = float(rows * plan.devices)
    view_total = float(views * plan.devices)
    image_total = float(views * plan.devices // 2)
    dp_me, fsdp_me = lax.axis_index(DP), lax.axis_index(FSDP)
    y_me, c_me = dp_me // 2, dp_me % 2
    z_me, x_me = fsdp_me // 2, fsdp_me % 2
    y_other, c_other, x_other = 1 - y_me, 1 - c_me, 1 - x_me

    barrier = pltpu.get_barrier_semaphore()

    @pl.loop(1, plan.dp)
    def _(step):
        pl.semaphore_signal(
            barrier, 1, device_id={DP: lax.rem(dp_me + step, plan.dp)}, device_id_type=pl.DeviceIdType.MESH
        )

    @pl.loop(1, plan.fsdp)
    def _(step):
        pl.semaphore_signal(
            barrier, 1, device_id={FSDP: lax.rem(fsdp_me + step, plan.fsdp)}, device_id_type=pl.DeviceIdType.MESH
        )

    pl.semaphore_wait(barrier, plan.dp + plan.fsdp - 2)

    def share(axis, size, me, source_of, slots, send, recv):
        def outgoing(step):
            partner = lax.rem(me + step, size)
            return pltpu.make_async_remote_copy(
                src_ref=source_of(partner),
                dst_ref=slots.at[me],
                send_sem=send.at[step],
                recv_sem=recv.at[me],
                device_id={axis: partner},
                device_id_type=pl.DeviceIdType.MESH,
            )

        def incoming(step):
            source = lax.rem(me + step, size)
            return pltpu.make_async_remote_copy(
                src_ref=slots.at[source],
                dst_ref=slots.at[source],
                send_sem=send.at[step],
                recv_sem=recv.at[source],
                device_id={axis: source},
                device_id_type=pl.DeviceIdType.MESH,
            )

        def start():
            pl.loop(1, size)(lambda step: outgoing(step).start())

        def wait():
            pl.loop(1, size)(lambda step: incoming(step).wait_recv())
            pl.loop(1, size)(lambda step: outgoing(step).wait_send())

        return start, wait

    def add_slots(slots, size):
        total = slots[0]
        for place in range(1, size):
            total = total + slots[place]
        return total

    class Sum:
        def __init__(self, which):
            part = mem.sums[which if which < 4 else (3, 2, 0, 1, 4)[which - 4]]
            self.dp_slots, self.fsdp_slots = part.dp, part.fsdp
            self.dp_copy = share(
                DP, plan.dp, dp_me, lambda _: self.dp_slots.at[dp_me], self.dp_slots, part.s0, part.r0
            )
            self.fsdp_copy = share(
                FSDP, plan.fsdp, fsdp_me, lambda _: self.fsdp_slots.at[fsdp_me], self.fsdp_slots, part.s1, part.r1
            )

        def start(self, *values):
            for place, value in enumerate(values):
                self.dp_slots[dp_me, place : place + 1, :] = value
            self.dp_copy[0]()

        def middle(self):
            self.dp_copy[1]()
            self.fsdp_slots[fsdp_me] = add_slots(self.dp_slots, plan.dp)
            self.fsdp_copy[0]()

        def finish(self):
            self.fsdp_copy[1]()
            return add_slots(self.fsdp_slots, plan.fsdp)

        def all(self, *values):
            self.start(*values)
            self.middle()
            return self.finish()

    def sum_matrix(which, matrix, extra):
        part = mem.mats[which]
        size = plan.embed_rows
        pack = part.pack
        flat = jnp.concatenate(
            [matrix] + extra + [jnp.zeros((size * plan.dp - P_OUT - len(extra), P_OUT), f32)], axis=0
        )
        for place in range(plan.dp):
            pack[place] = flat[place * size : (place + 1) * size]
        start, wait = share(DP, plan.dp, dp_me, lambda to: pack.at[to], part.dp, part.s0, part.r0)
        start()
        part.dp[dp_me] = pack[dp_me]
        wait()
        part.fsdp[fsdp_me] = add_slots(part.dp, plan.dp)
        start, wait = share(
            FSDP, plan.fsdp, fsdp_me, lambda _: part.fsdp.at[fsdp_me], part.fsdp, part.s1, part.r1
        )
        start()
        wait()
        part.all[dp_me] = add_slots(part.fsdp, plan.fsdp)
        start, wait = share(
            DP, plan.dp, dp_me, lambda _: part.all.at[dp_me], part.all, part.s2, part.r2
        )
        start()
        wait()
        total = jnp.concatenate([part.all[place] for place in range(plan.dp)], axis=0)
        return total[:P_OUT], [total[P_OUT + place : P_OUT + place + 1] for place in range(len(extra))]

    weights = mem.w
    everything = slice(None)

    def row_span(which, half):
        size = plan.half[which]
        if half is None:
            return 0, 2 * size
        return half * size, size

    def column_span(which, dp_index):
        width = plan.width[which]
        return pl.ds(pl.multiple_of(dp_index * width, width), width)

    def places(which, z_index, x_index, dp_index, half):
        start, size = row_span(which, half)
        if which == 1:
            z_list = range(plan.z) if z_index is None else [z_index]
            x_list = range(plan.x) if x_index is None else [x_index]
            return [
                (
                    pl.ds(pl.multiple_of((z_one * plan.x + x_one) * 576 + start, 16), size),
                    column_span(which, dp_index),
                )
                for z_one in z_list
                for x_one in x_list
            ]
        z_one = everything if z_index is None else z_index
        x_one = everything if x_index is None else x_index
        if which == 2:
            return [(dp_index, z_one, x_one, pl.ds(start, size), everything)]
        if which == 4:
            return [(z_one, x_one, pl.ds(pl.multiple_of(dp_index * 32 + start, 16), size), everything)]
        return [(z_one, x_one, pl.ds(start, size), column_span(which, dp_index))]

    recv_parts = {
        1: lambda index: mem.h3.at[index],
        0: lambda index: mem.r4.at[index],
        2: lambda index: mem.r3.at[index],
        3: lambda index: mem.r4.at[index],
        4: lambda index: mem.r5.at[index],
    }

    counter = [0]

    class Batch:
        def __init__(self, sources, targets, landings, axis, partner):
            base = counter[0]
            counter[0] += len(sources)
            send, recv = mem.bulk_send, mem.bulk_recv
            self.out = [
                pltpu.make_async_remote_copy(
                    src_ref=source,
                    dst_ref=target,
                    send_sem=send.at[base + place],
                    recv_sem=recv.at[base + place],
                    device_id={axis: partner},
                    device_id_type=pl.DeviceIdType.MESH,
                )
                for place, (source, target) in enumerate(zip(sources, targets))
            ]
            self.come = [
                pltpu.make_async_remote_copy(
                    src_ref=landing,
                    dst_ref=landing,
                    send_sem=send.at[base + place],
                    recv_sem=recv.at[base + place],
                    device_id={axis: partner},
                    device_id_type=pl.DeviceIdType.MESH,
                )
                for place, landing in enumerate(landings)
            ]

        def start(self):
            for copy in self.out:
                copy.start()

        def arrive(self):
            for copy in self.come:
                copy.wait_recv()

        def leave(self):
            for copy in self.out:
                copy.wait_send()

    class LineBatch:
        def __init__(self, source_of, target_of, landing_of):
            base = counter[0]
            counter[0] += plan.z
            send, recv = mem.bulk_send, mem.bulk_recv
            self.out, self.come = [], []
            for step in range(1, plan.z):
                z_to = (z_me + step) % plan.z
                self.out.append(
                    pltpu.make_async_remote_copy(
                        src_ref=source_of(z_to),
                        dst_ref=target_of(z_to),
                        send_sem=send.at[base + step],
                        recv_sem=recv.at[base + z_me],
                        device_id={FSDP: z_to * plan.x + x_me},
                        device_id_type=pl.DeviceIdType.MESH,
                    )
                )
                self.come.append(
                    pltpu.make_async_remote_copy(
                        src_ref=landing_of(z_to),
                        dst_ref=landing_of(z_to),
                        send_sem=send.at[base + step],
                        recv_sem=recv.at[base + z_to],
                        device_id={FSDP: z_to * plan.x + x_me},
                        device_id_type=pl.DeviceIdType.MESH,
                    )
                )

        start, arrive, leave = Batch.start, Batch.arrive, Batch.leave

    def pick(ref, indexes):
        return [ref.at[index] for index in indexes]

    def own_dp(y_index, c_index):
        return y_index * 2 + c_index

    x_partner = z_me * plan.x + x_other
    y_partner = own_dp(y_other, c_me)
    c_partner = own_dp(y_me, c_other)
    dp_far = own_dp(y_other, c_other)

    class Gather:
        def __init__(self, which):
            ref = weights[which]
            self.which = which

            def at(*index):
                return pick(ref, places(which, *index))

            own = at(z_me, x_me, dp_me, None)[0]
            self.line = LineBatch(
                lambda _: own, lambda _: own, lambda z_from: at(z_from, x_me, dp_me, None)[0]
            )
            sent, come = at(None, x_me, dp_me, 0), at(None, x_other, dp_me, 0)
            self.x_first = Batch(sent, sent, come, FSDP, x_partner)
            sent, come = at(None, x_me, dp_me, 1), at(None, x_me, y_partner, 1)
            self.y_first = Batch(sent, sent, come, DP, y_partner)
            sent, come = at(None, None, dp_me, 0), at(None, None, y_partner, 0)
            self.y_second = Batch(sent, sent, come, DP, y_partner)
            sent = at(None, x_me, dp_me, 1) + at(None, x_me, y_partner, 1)
            come = at(None, x_other, dp_me, 1) + at(None, x_other, y_partner, 1)
            self.x_second = Batch(sent, sent, come, FSDP, x_partner)
            sent = at(None, None, dp_me, None) + at(None, None, y_partner, None)
            come = at(None, None, c_partner, None) + at(None, None, dp_far, None)
            self.core = Batch(sent, sent, come, DP, c_partner)
            self.stages = ((self.line,), (self.x_first, self.y_first), (self.y_second, self.x_second), (self.core,))

        def put_own(self, value):
            weights[self.which][places(self.which, z_me, x_me, dp_me, None)[0]] = value.astype(bf16)

        def start(self, stage):
            if plan.inside:
                for batch in self.stages[stage]:
                    batch.start()

        def arrive(self, stage):
            if plan.inside:
                for batch in self.stages[stage]:
                    batch.arrive()

        def step(self, stage):
            self.arrive(stage)
            self.start(stage + 1)

        def leave(self):
            if plan.inside:
                for stage in self.stages:
                    for batch in stage:
                        batch.leave()

    class Piece:
        def __init__(self, which, ref, room, z_index):
            def at(*index):
                return pick(ref, places(which, z_index, *index))

            def land(*index):
                return [room(index_one) for index_one in places(which, z_index, *index)]

            self.z = z_index
            self.core = Batch(
                at(None, c_partner, None) + at(None, dp_far, None),
                land(None, c_partner, None) + land(None, dp_far, None),
                land(None, dp_me, None) + land(None, y_partner, None),
                DP,
                c_partner,
            )
            self.y_first = Batch(
                at(None, y_partner, 0), land(None, dp_far, 0), land(None, c_partner, 0), DP, y_partner
            )
            self.x_first = Batch(
                at(x_other, dp_me, 1) + at(x_other, y_partner, 1),
                land(x_other, c_partner, 1) + land(x_other, dp_far, 1),
                land(x_me, c_partner, 1) + land(x_me, dp_far, 1),
                FSDP,
                x_partner,
            )
            self.x_second = Batch(
                at(x_other, dp_me, 0), land(x_other, dp_far, 0), land(x_me, dp_far, 0), FSDP, x_partner
            )
            self.y_second = Batch(
                at(x_me, y_partner, 1), land(x_other, dp_far, 1), land(x_other, c_partner, 1), DP, y_partner
            )

    class Reduce:
        def __init__(self, which, ref, cut):
            self.which, self.ref, self.room = which, ref, recv_parts[which]
            self.pieces = [
                Piece(which, ref, self.room, z_index) for z_index in (range(plan.z) if cut else [None])
            ]
            self.base = counter[0]
            counter[0] += plan.z

        def line_copy(self, z_to):
            return pltpu.make_async_remote_copy(
                src_ref=self.ref.at[places(self.which, z_to, x_me, dp_me, None)[0]],
                dst_ref=self.room(places(self.which, z_me, x_other, dp_far, None)[0]),
                send_sem=mem.bulk_send.at[self.base + z_to],
                recv_sem=mem.bulk_recv.at[self.base + z_me],
                device_id={FSDP: z_to * plan.x + x_me},
                device_id_type=pl.DeviceIdType.MESH,
            )

        def line_room(self, z_from):
            return self.room(places(self.which, z_from, x_other, dp_far, None)[0])

        def add(self, z_index, pairs):
            def one(z_one):
                for here, there in pairs:
                    for x_step in range(plan.x) if here[0] is None else [None]:
                        x_here = x_step if here[0] is None else here[0]
                        x_there = x_step if there[0] is None else there[0]
                        index = places(self.which, z_one, x_here, *here[1:])[0]
                        other = places(self.which, z_one, x_there, *there[1:])[0]
                        total = self.ref[index].astype(f32) + self.room(other)[...].astype(f32)
                        self.ref[index] = total.astype(bf16)

            if z_index is None:
                pl.loop(0, plan.z)(one)
            else:
                one(z_index)

        def core_start(self, place=0):
            if plan.inside:
                self.pieces[place].core.start()

        def core_add(self, place=0):
            if plan.inside:
                piece = self.pieces[place]
                piece.core.arrive()
                self.add(piece.z, [((None, dp_me, None),) * 2, ((None, y_partner, None),) * 2])
                piece.y_first.start()
                piece.x_first.start()

        def first_add(self, place=0):
            if plan.inside:
                piece = self.pieces[place]
                piece.y_first.arrive()
                self.add(piece.z, [((None, dp_me, 0), (None, c_partner, 0))])
                piece.x_second.start()
                piece.x_first.arrive()
                self.add(
                    piece.z, [((x_me, dp_me, 1), (x_me, c_partner, 1)), ((x_me, y_partner, 1), (x_me, dp_far, 1))]
                )
                piece.y_second.start()

        def second_add(self, place=0):
            if plan.inside:
                piece = self.pieces[place]
                piece.x_second.arrive()
                piece.y_second.arrive()
                self.add(
                    piece.z, [((x_me, dp_me, 0), (x_me, dp_far, 0)), ((x_me, dp_me, 1), (x_other, c_partner, 1))]
                )
                if piece.z is None:
                    for step in range(1, plan.z):
                        self.line_copy((z_me + step) % plan.z).start()
                else:

                    @pl.when(z_me != piece.z)
                    def _():
                        self.line_copy(piece.z).start()

        def finish(self):
            if not plan.inside:
                return
            total = self.ref[places(self.which, z_me, x_me, dp_me, None)[0]].astype(f32)
            for step in range(1, plan.z):
                z_from = (z_me + step) % plan.z
                room = self.line_room(z_from)
                pltpu.make_async_remote_copy(
                    src_ref=room,
                    dst_ref=room,
                    send_sem=mem.bulk_send.at[self.base + z_from],
                    recv_sem=mem.bulk_recv.at[self.base + z_from],
                    device_id={FSDP: z_from * plan.x + x_me},
                    device_id_type=pl.DeviceIdType.MESH,
                ).wait_recv()
                total = total + room[...].astype(f32)
            outs.grads[self.which][...] = total
            squares = jnp.sum(total * total, axis=0, keepdims=True)
            folded = squares[:, :LANES]
            for place in range(1, squares.shape[1] // LANES):
                folded = folded + squares[:, place * LANES : (place + 1) * LANES]
            mem.squares[...] += folded
            for step in range(1, plan.z):
                self.line_copy((z_me + step) % plan.z).wait_send()
            for piece in self.pieces:
                for batch in (piece.core, piece.y_first, piece.x_first, piece.x_second, piece.y_second):
                    batch.leave()

    gathers = [Gather(which) for which in range(5)]
    gradients = [weights[0], mem.stage.at[pl.ds(0, 9 * C_MID)], weights[2], weights[3], weights[4]]
    reduces = [Reduce(which, gradients[which], which < 2) for which in range(5)]
    mem.squares[...] = jnp.zeros((1, LANES), f32)

    if plan.inside:
        for which in range(5):
            gathers[which].put_own(ins.shards[which][...])
            gathers[which].start(0)
        tiles = mem.norm_tiles
        tiles[dp_me, fsdp_me] = ins.norm[...].astype(bf16).astype(f32)
        norm_dp = share(
            DP, plan.dp, dp_me, lambda _: tiles.at[dp_me, fsdp_me], tiles.at[:, fsdp_me], mem.norm_s0, mem.norm_r0
        )
        norm_dp[0]()
    else:
        loads = [
            pltpu.make_async_copy(ins.shards[which], weights[which], mem.bulk_send.at[which])
            for which in range(5)
        ]
        for load in loads:
            load.start()

    stage_ref, stage_sem = mem.stage, mem.stage_sem
    slot_rows = BLOCKS * chunk

    def chunk_rows(slot, block):
        return pl.ds(pl.multiple_of(slot * slot_rows + block * chunk, 16), chunk)

    def chunk_copies(array, index, into):
        slot = lax.rem(index, 3)
        copies = []
        for block in range(BLOCKS):
            outer = array.at[pl.ds(pl.multiple_of(index * chunk, 16), chunk), pl.ds(block * C_MID, C_MID)]
            inner = stage_ref.at[chunk_rows(slot, block)]
            source, target = (outer, inner) if into else (inner, outer)
            copies.append(pltpu.make_async_copy(source, target, stage_sem.at[0 if into else 1, slot, block]))
        return copies

    def load(array, index):
        for copy in chunk_copies(array, index, True):
            copy.start()

    def load_wait(array, index):
        for copy in chunk_copies(array, index, True):
            copy.wait()

    def save(array, index):
        for copy in chunk_copies(array, index, False):
            copy.start()

    def save_wait(array, index):
        for copy in chunk_copies(array, index, False):
            copy.wait()

    features, slope_hbm = ins.features, outs.slope
    load(features, 0)
    load(features, 1)

    padded_one, padded_two = mem.pad1, mem.pad2
    for padded in (padded_one, padded_two):
        for edge in (0, SIDE + 1):
            padded[edge] = jnp.zeros((padded.shape[1], C_MID), bf16)
        for edge in (0, SIDE + 1):
            padded[:, pl.ds(edge * views, views), :] = jnp.zeros((SIDE + 2, views, C_MID), bf16)

    if plan.inside:
        norm_dp[1]()
        norm_out = []
        norm_in = []
        for step in range(1, plan.fsdp):
            partner = (fsdp_me + step) % plan.fsdp
            norm_out.append(
                pltpu.make_async_remote_copy(
                    src_ref=tiles.at[:, fsdp_me],
                    dst_ref=tiles.at[:, fsdp_me],
                    send_sem=mem.norm_s1.at[step],
                    recv_sem=mem.norm_r1.at[fsdp_me],
                    device_id={FSDP: partner},
                    device_id_type=pl.DeviceIdType.MESH,
                )
            )
            norm_in.append(
                pltpu.make_async_remote_copy(
                    src_ref=tiles.at[:, partner],
                    dst_ref=tiles.at[:, partner],
                    send_sem=mem.norm_s1.at[step],
                    recv_sem=mem.norm_r1.at[partner],
                    device_id={FSDP: partner},
                    device_id_type=pl.DeviceIdType.MESH,
                )
            )
        for copy in norm_out:
            copy.start()
        gathers[0].step(0)
        gathers[0].step(1)
        gathers[0].step(2)
        gathers[1].step(0)
        gathers[0].arrive(3)
        for copy in norm_in:
            copy.wait_recv()
        for copy in norm_out:
            copy.wait_send()
        norm_all = mem.norm
        for dp_one in range(plan.dp):
            for fsdp_one in range(plan.fsdp):
                start = (dp_one * plan.fsdp + fsdp_one) * LANES
                norm_all[:, start : start + LANES] = tiles[dp_one, fsdp_one]
    else:
        for copy in loads:
            copy.wait()
        norm_all = mem.norm
        norm_all[...] = ins.norm[...]

    starts = (0, C_MID, 2 * C_MID, 2 * C_MID + C_IN, 2 * C_MID + C_IN + P_HID)

    def gain(layer):
        return norm_all[0:1, starts[layer] : starts[layer + 1]]

    def shift(layer):
        return norm_all[1:2, starts[layer] : starts[layer + 1]]

    coef, stats = mem.coef, mem.stats

    def norm_coefs(layer, totals, count):
        width = starts[layer + 1] - starts[layer]
        mean = totals[0:1] / count
        scaling = lax.rsqrt(totals[1:2] / count - mean * mean + norm_epsilon)
        slope = scaling * gain(layer)
        stats[0:1, starts[layer] : starts[layer + 1]] = mean
        stats[1:2, starts[layer] : starts[layer + 1]] = scaling
        coef[0:1, :width] = slope
        coef[1:2, :width] = shift(layer) - mean * slope

    def grad_coefs(layer, totals, count):
        width = starts[layer + 1] - starts[layer]
        mean = stats[0:1, starts[layer] : starts[layer + 1]]
        scaling = stats[1:2, starts[layer] : starts[layer + 1]]
        outs.norm_grad[0:1, starts[layer] : starts[layer + 1]] = totals[1:2]
        outs.norm_grad[1:2, starts[layer] : starts[layer + 1]] = totals[0:1]
        slope = scaling * gain(layer)
        bend = slope * scaling * totals[1:2] / count
        coef[0:1, :width] = slope
        coef[1:2, :width] = slope * totals[0:1] / count - mean * bend
        coef[2:3, :width] = bend

    def xhat_sum(layer, plain, product):
        mean = stats[0:1, starts[layer] : starts[layer + 1]]
        scaling = stats[1:2, starts[layer] : starts[layer + 1]]
        return scaling * (product - mean * plain)

    zero_row = jnp.zeros((1, C_MID), f32)

    def at_chunk(index, place, *moves):
        if plan.inside:

            @pl.when(index == place)
            def _():
                for move in moves:
                    move()

    def column_sums(value):
        return jnp.sum(value, axis=0, keepdims=True)

    def whole(which):
        value = weights[which][...]
        return value.reshape(-1, value.shape[-1])

    def stage_chunk(index):
        slot = lax.rem(index, 3)
        return jnp.concatenate([stage_ref[chunk_rows(slot, block), :] for block in range(BLOCKS)], axis=1)

    def span(index):
        return pl.ds(pl.multiple_of(index * chunk, 16), chunk)

    hidden_one, slope_one = mem.h1, mem.d1
    hidden_two, slope_two = mem.h2, mem.d2
    act_two = mem.a2
    hidden_three = mem.h3

    def first_body(index, sums):
        load_wait(features, index)

        @pl.when(index + 2 < CHUNKS)
        def _():
            load(features, index + 2)

        hidden = dot(stage_chunk(index), whole(0))
        hidden_one[span(index), :] = hidden.astype(bf16)
        at_chunk(index, 4, lambda: gathers[1].step(1))
        return sums[0] + column_sums(hidden), sums[1] + column_sums(hidden * hidden)

    sums = lax.fori_loop(0, CHUNKS, first_body, (zero_row, zero_row))
    sum_one = Sum(0)
    sum_one.start(*sums)
    gathers[2].step(0)
    sum_one.middle()
    load(features, 0)
    load(features, 1)
    norm_coefs(0, sum_one.finish(), row_total)

    def activate(hidden_ref, slope_ref, put):
        @pl.loop(0, PIX)
        def _(pixel):
            place = pl.ds(pl.multiple_of(pixel * views, 16), views)
            for block in range(C_MID // LANES):
                cols = slice(block * LANES, (block + 1) * LANES)
                out = hidden_ref[place, cols].astype(f32) * coef[0:1, cols] + coef[1:2, cols]
                value, slope = gelu_pair(out)
                slope_ref[place, cols] = slope.astype(bf16)
                put(pixel, cols, value.astype(bf16))

    def put_padded(padded):
        def put(pixel, cols, value):
            padded[pixel // SIDE + 1, pl.ds(pl.multiple_of((pixel % SIDE + 1) * views, 16), views), cols] = value

        return put

    activate(hidden_one, slope_one, put_padded(padded_one))
    gathers[1].step(2)
    gathers[3].step(0)
    gathers[1].arrive(3)

    def patch(padded, index, flip):
        pieces = []
        for vertical in range(3):
            for lateral in range(3):
                down, across = (2 - vertical, 2 - lateral) if flip else (vertical, lateral)
                pieces.append(padded[index + down, across * views : across * views + chunk, :])
        return jnp.concatenate(pieces, axis=1)

    def second_body(index, sums):
        hidden = dot(patch(padded_one, index, False), weights[1][...])
        hidden_two[span(index), :] = hidden.astype(bf16)
        at_chunk(index, 0, lambda: gathers[2].step(1))
        at_chunk(index, 2, lambda: gathers[4].step(0), lambda: gathers[2].step(2))
        at_chunk(index, 4, lambda: gathers[3].step(1), lambda: gathers[4].step(1))
        return sums[0] + column_sums(hidden), sums[1] + column_sums(hidden * hidden)

    sums = lax.fori_loop(0, CHUNKS, second_body, (zero_row, zero_row))
    sum_two = Sum(1)
    sum_two.start(*sums)
    sum_two.middle()
    norm_coefs(1, sum_two.finish(), row_total)

    def put_rows(pixel, cols, value):
        act_two[pl.ds(pl.multiple_of(pixel * views, 16), views), cols] = value

    activate(hidden_two, slope_two, put_rows)
    gathers[2].arrive(3)

    def block_rows(block, index):
        return pl.ds(pl.multiple_of(block * rows + index * chunk, 16), chunk)

    def weight_three(block):
        return weights[2][block].reshape(C_MID, C_MID)

    def third_body(index, sums):
        left = act_two[span(index), :]
        result = []
        for block in range(BLOCKS):
            hidden = dot(left, weight_three(block))
            hidden_three[block_rows(block, index), :] = hidden.astype(bf16)
            result.append(
                (sums[block][0] + column_sums(hidden), sums[block][1] + column_sums(hidden * hidden))
            )
        at_chunk(index, 4, lambda: gathers[3].step(2), lambda: gathers[4].step(2))
        return tuple(result)

    sums = lax.fori_loop(0, CHUNKS, third_body, ((zero_row, zero_row),) * BLOCKS)
    sum_three = Sum(2)
    sum_three.start(
        jnp.concatenate([pair[0] for pair in sums], axis=1), jnp.concatenate([pair[1] for pair in sums], axis=1)
    )
    sum_three.middle()
    gathers[4].arrive(3)
    norm_coefs(2, sum_three.finish(), row_total)

    pool, pool_slope, pool_bend = mem.pool, mem.pool_slope, mem.pool_bend
    for ref in (pool, pool_slope, pool_bend):
        ref[...] = jnp.zeros_like(ref)

    def pool_body(index, carry):
        load_wait(features, index)
        slot = lax.rem(index, 3)
        for block in range(BLOCKS):

            @pl.loop(0, C_MID // LANES)
            def _(part):
                inner = pl.ds(pl.multiple_of(part * LANES, LANES), LANES)
                cols = pl.ds(pl.multiple_of(block * C_MID + part * LANES, LANES), LANES)
                slope_row, shift_row = coef[0:1, cols], coef[1:2, cols]
                kept = (pool[:, cols], pool_slope[:, cols], pool_bend[:, cols])
                for pixel in range(SIDE):
                    stage_at = pl.ds(
                        pl.multiple_of(slot * slot_rows + block * chunk + pixel * views, 16), views
                    )
                    hidden_at = pl.ds(
                        pl.multiple_of(block * rows + index * chunk + pixel * views, 16), views
                    )
                    hidden = hidden_three[hidden_at, inner].astype(f32)
                    total = hidden * slope_row + shift_row + stage_ref[stage_at, inner].astype(f32)
                    value, slope = gelu_pair(total)
                    stage_ref[stage_at, inner] = slope.astype(bf16)
                    kept = (kept[0] + value, kept[1] + slope, kept[2] + slope * hidden)
                pool[:, cols], pool_slope[:, cols], pool_bend[:, cols] = kept

        save(slope_hbm, index)

        @pl.when(index >= 1)
        def _():
            save_wait(slope_hbm, index - 1)

        @pl.when(index + 2 < CHUNKS)
        def _():
            load(features, index + 2)

        return carry

    lax.fori_loop(0, CHUNKS, pool_body, 0)
    save_wait(slope_hbm, CHUNKS - 1)
    gathers[3].arrive(3)
    for one in gathers:
        one.leave()

    pooled = (pool[...] * (1.0 / PIX)).astype(bf16)
    mem.pooled[...] = pooled
    proj_hidden = dot(pooled, whole(3))
    sum_four = Sum(3)
    totals = sum_four.all(column_sums(proj_hidden), column_sums(proj_hidden * proj_hidden))
    load(slope_hbm, 0)
    load(slope_hbm, 1)
    norm_coefs(3, totals, view_total)
    value, slope = gelu_pair(proj_hidden * coef[0:1, :P_HID] + coef[1:2, :P_HID])
    proj_act = value.astype(bf16)
    mem.proj_act[...] = proj_act
    mem.proj_slope[...] = slope
    mem.proj_hidden[...] = proj_hidden

    def weight_five(block):
        return weights[4][block // plan.x, block % plan.x]

    parts = P_HID // P_OUT
    embedding = jnp.zeros((views, P_OUT), f32)
    for block in range(parts):
        embedding = embedding + dot_cols(proj_act[:, block * P_OUT : (block + 1) * P_OUT], weight_five(block))

    images = views // 2
    order = jnp.broadcast_to(ins.order[...], (images, views))
    image_row = lax.broadcasted_iota(jnp.int32, (images, views), 0)
    selectors = [(order == 2 * image_row + which).astype(f32) for which in range(2)]
    embeds = [exact_dot(selector, embedding) for selector in selectors]
    moments = [exact_rows(embed, embed) for embed in embeds]
    packed, diagonal = pack_pair(*moments)
    packed, extra = sum_matrix(0, packed, [diagonal] + [column_sums(embed) for embed in embeds])
    moments = unpack_pair(packed, extra[0])
    eye = (
        lax.broadcasted_iota(jnp.int32, (P_OUT, P_OUT), 0) == lax.broadcasted_iota(jnp.int32, (P_OUT, P_OUT), 1)
    ).astype(f32)
    centred, covariances = [], []
    for which in range(2):
        mean = extra[1 + which] / image_total
        centred.append(embeds[which] - mean)
        covariances.append(moments[which] / image_total - exact_rows(mean, mean) + ridge_term * eye)
    inverses = inverse_factors(covariances)
    whitened = [exact_cols(centred[which], inverses[which]) for which in range(2)]
    scalings = [
        lax.rsqrt(jnp.mean(white * white, axis=1, keepdims=True) + norm_epsilon) for white in whitened
    ]
    units = [white * scaling for white, scaling in zip(whitened, scalings)]
    difference = units[0] - units[1]
    objective_row = column_sums(difference * difference) * (1.0 / P_OUT)
    unit_grads = [difference * (2.0 / P_OUT), difference * (-2.0 / P_OUT)]
    white_grads = []
    for which in range(2):
        inner = jnp.mean(whitened[which] * unit_grads[which], axis=1, keepdims=True)
        white_grads.append(
            scalings[which] * unit_grads[which] - whitened[which] * (scalings[which] ** 3 * inner)
        )
    directs = [exact_dot(white_grads[which], inverses[which]) for which in range(2)]
    products = [exact_rows(white_grads[which], whitened[which]) for which in range(2)]
    packed, diagonal = pack_pair(*products)
    packed, extra = sum_matrix(
        1, packed, [diagonal] + [column_sums(grad) for grad in white_grads] + [objective_row]
    )
    products = unpack_pair(packed, extra[0])
    embed_grad = jnp.zeros((views, P_OUT), f32)
    for which in range(2):
        symmetric = exact_rows(inverses[which], exact_dot(products[which], inverses[which]))
        mean_grad = exact_dot(extra[1 + which], inverses[which])
        grad = directs[which] - (exact_dot(centred[which], symmetric) + mean_grad) / image_total
        embed_grad = embed_grad + exact_rows(selectors[which], grad)
    objective_row = extra[3]
    embed_low = embed_grad.astype(bf16)

    proj_act, proj_hidden = mem.proj_act[...], mem.proj_hidden[...]
    act_grad = jnp.concatenate([dot(embed_low, weight_five(block)) for block in range(parts)], axis=1)
    upstream = act_grad * mem.proj_slope[...]
    plain = column_sums(upstream)
    sum_four_back = Sum(4)
    sum_four_back.start(plain, xhat_sum(3, plain, column_sums(upstream * proj_hidden)))
    for block in range(parts):
        weights[4][block // plan.x, block % plan.x] = dot_rows(
            embed_low, proj_act[:, block * P_OUT : (block + 1) * P_OUT]
        ).astype(bf16)
    sum_four_back.middle()
    reduces[4].core_start()
    grad_coefs(3, sum_four_back.finish(), view_total)
    four_low = (
        upstream * coef[0:1, :P_HID] - coef[1:2, :P_HID] - proj_hidden * coef[2:3, :P_HID]
    ).astype(bf16)
    pool_grad = dot_cols(four_low, whole(3)) * (1.0 / PIX)
    plain = column_sums(pool_grad * pool_slope[...])
    sum_three_back = Sum(5)
    sum_three_back.start(plain, xhat_sum(2, plain, column_sums(pool_grad * pool_bend[...])))
    grad_four = dot_rows(mem.pooled[...], four_low).astype(bf16)
    weights[3][...] = grad_four.reshape(weights[3].shape)
    sum_three_back.middle()
    reduces[3].core_start()
    grad_coefs(2, sum_three_back.finish(), row_total)
    pool[...] = pool_grad * coef[0:1, :]
    pool_slope[...] = pool_grad
    pool_copy = pltpu.make_async_copy(pool_slope, outs.pool_grad, mem.column_sem.at[BLOCKS + 2])
    pool_copy.start()

    def third_back(index, sums):
        load_wait(slope_hbm, index)

        @pl.when(index + 2 < CHUNKS)
        def _():
            load(slope_hbm, index + 2)

        slot = lax.rem(index, 3)
        for block in range(BLOCKS):

            @pl.loop(0, C_MID // LANES)
            def _(part):
                inner = pl.ds(pl.multiple_of(part * LANES, LANES), LANES)
                cols = pl.ds(pl.multiple_of(block * C_MID + part * LANES, LANES), LANES)
                spread, shift_row, bend_row = pool[:, cols], coef[1:2, cols], coef[2:3, cols]
                for pixel in range(SIDE):
                    stage_at = pl.ds(
                        pl.multiple_of(slot * slot_rows + block * chunk + pixel * views, 16), views
                    )
                    hidden_at = pl.ds(
                        pl.multiple_of(block * rows + index * chunk + pixel * views, 16), views
                    )
                    hidden = hidden_three[hidden_at, inner].astype(f32)
                    grad = stage_ref[stage_at, inner].astype(f32) * spread - shift_row - hidden * bend_row
                    hidden_three[hidden_at, inner] = grad.astype(bf16)

        at_chunk(index, 0, reduces[4].core_add)
        at_chunk(index, 1, reduces[3].core_add)
        at_chunk(index, 2, reduces[4].first_add)
        at_chunk(index, 4, reduces[4].second_add)
        at_chunk(index, 6, reduces[3].first_add)
        left = jnp.concatenate([hidden_three[block_rows(block, index), :] for block in range(BLOCKS)], axis=1)
        right = jnp.concatenate([weight_three(block) for block in range(BLOCKS)], axis=1)
        upstream = dot_cols(left, right) * slope_two[span(index), :].astype(f32)
        slope_two[span(index), :] = upstream.astype(bf16)
        return (
            sums[0] + column_sums(upstream),
            sums[1] + column_sums(upstream * hidden_two[span(index), :].astype(f32)),
        )

    sums = lax.fori_loop(0, CHUNKS, third_back, (zero_row, zero_row))
    sum_two_back = Sum(6)
    sum_two_back.start(sums[0], xhat_sum(1, *sums))
    for block in range(BLOCKS):
        grad = dot_rows(act_two[...], hidden_three[block * rows : (block + 1) * rows, :])
        weights[2][block] = grad.astype(bf16).reshape(plan.z, plan.x, -1, C_MID)
        if block == 1:
            sum_two_back.middle()
    reduces[2].core_start()
    reduces[3].second_add()
    grad_coefs(1, sum_two_back.finish(), row_total)

    def apply_grad(hidden_ref, grad_ref, put):
        @pl.loop(0, PIX)
        def _(pixel):
            place = pl.ds(pl.multiple_of(pixel * views, 16), views)
            for block in range(C_MID // LANES):
                cols = slice(block * LANES, (block + 1) * LANES)
                grad = (
                    grad_ref[place, cols].astype(f32) * coef[0:1, cols]
                    - coef[1:2, cols]
                    - hidden_ref[place, cols].astype(f32) * coef[2:3, cols]
                )
                put(pixel, cols, grad.astype(bf16))

    apply_grad(hidden_two, slope_two, put_padded(padded_two))
    reduces[4].finish()
    reduces[2].core_add()

    feature_rows = (2 * rows, 3 * rows)

    def columns_copy(block):
        return pltpu.make_async_copy(
            features.at[:, pl.ds(block * C_MID, C_MID)],
            hidden_three.at[pl.ds(feature_rows[block % 2], rows)],
            mem.column_sem.at[block],
        )

    def tap_grad(tap):
        down, across = tap // 3, tap % 3
        left = padded_one[pl.ds(down, SIDE), pl.ds(pl.multiple_of(across * views, 16), chunk), :]
        right = padded_two[1 : SIDE + 1, views : views + chunk, :]
        grad = dot_rows(left.reshape(rows, C_MID), right.reshape(rows, C_MID))
        mem.stage[pl.ds(pl.multiple_of(tap * C_MID, 16), C_MID), :] = grad.astype(bf16)

    pl.loop(0, 3)(tap_grad)
    reduces[1].core_start(0)
    reduces[2].first_add()
    pl.loop(3, 5)(tap_grad)
    reduces[1].core_start(1)
    reduces[1].core_add(0)
    reduces[3].finish()
    pl.loop(5, 7)(tap_grad)
    reduces[1].core_start(2)
    reduces[1].core_add(1)
    reduces[2].second_add()
    reduces[1].first_add(0)
    pl.loop(7, 9)(tap_grad)
    reduces[1].core_start(3)
    reduces[1].core_add(2)
    reduces[1].first_add(1)

    def second_back(index, sums):
        right = jnp.concatenate([weights[1][tap * C_MID : (tap + 1) * C_MID, :] for tap in range(9)], axis=1)
        upstream = dot_cols(patch(padded_two, index, True), right) * slope_one[span(index), :].astype(f32)
        slope_one[span(index), :] = upstream.astype(bf16)
        at_chunk(index, 0, lambda: reduces[1].core_add(3), reduces[2].finish, lambda: reduces[1].second_add(0))
        at_chunk(index, 1, lambda: reduces[1].first_add(2))
        at_chunk(index, 2, lambda: reduces[1].second_add(1))
        at_chunk(index, 3, lambda: reduces[1].first_add(3), lambda: reduces[1].second_add(2))
        at_chunk(index, 5, lambda: reduces[1].second_add(3))
        return (
            sums[0] + column_sums(upstream),
            sums[1] + column_sums(upstream * hidden_one[span(index), :].astype(f32)),
        )

    sums = lax.fori_loop(0, CHUNKS, second_back, (zero_row, zero_row))
    sum_one_back = Sum(7)
    sum_one_back.start(sums[0], xhat_sum(0, *sums))
    columns_copy(0).start()
    columns_copy(1).start()
    weight_copy = pltpu.make_async_copy(weights[0], outs.low_one, mem.column_sem.at[BLOCKS])
    weight_copy.start()
    sum_one_back.middle()
    grad_coefs(0, sum_one_back.finish(), row_total)

    def put_one(pixel, cols, value):
        act_two[pl.ds(pl.multiple_of(pixel * views, 16), views), cols] = value

    apply_grad(hidden_one, slope_one, put_one)
    grad_copy = pltpu.make_async_copy(act_two, outs.one_low, mem.column_sem.at[BLOCKS + 1])
    grad_copy.start()
    weight_copy.wait()

    def block_grad(block):
        columns_copy(block).wait()
        start = feature_rows[block % 2]
        grad = dot_rows(hidden_three[start : start + rows, :], act_two[...])
        weights[0][block] = grad.astype(bf16).reshape(plan.x, -1, C_MID)
        if block + 2 < BLOCKS:
            columns_copy(block + 2).start()

    one = reduces[0]
    block_grad(0)
    one.core_start(0)
    block_grad(1)
    one.core_start(1)
    one.core_add(0)
    block_grad(2)
    one.core_start(2)
    one.core_add(1)
    one.first_add(0)
    reduces[1].finish()
    block_grad(3)
    one.core_start(3)
    one.core_add(2)
    one.first_add(1)
    one.second_add(0)
    one.core_add(3)
    one.first_add(2)
    one.second_add(1)
    one.first_add(3)
    one.second_add(2)
    one.second_add(3)
    one.finish()
    grad_copy.wait()
    pool_copy.wait()
    squares = mem.squares[...]
    norm_grads = outs.norm_grad[...]
    scalars = outs.scalars
    if plan.inside:
        squares = Sum(8).all(squares, squares)[0:1]
    norm_squares = column_sums(norm_grads * norm_grads)
    for place in range(norm_squares.shape[1] // LANES):
        squares = squares + norm_squares[:, place * LANES : (place + 1) * LANES]
    scalars[...] = jnp.zeros_like(scalars)
    scalars[0:1, :] = objective_row
    scalars[1:2, :] = squares
    if not plan.inside:
        stores = [
            pltpu.make_async_copy(gradients[which], outs.grads[which], mem.bulk_send.at[which])
            for which in range(5)
        ]
        for store in stores:
            store.start()
        for store in stores:
            store.wait()


def weight_shapes():
    return (
        (4, 2, 256, C_MID),
        (9 * C_MID, C_MID),
        (BLOCKS, 4, 2, 64, C_MID),
        (4, 2, 256, P_HID),
        (4, 2, P_OUT, P_OUT),
    )


def run_kernel(plan, features, order, shards, norm):
    rows, views = plan.rows, plan.views
    in_vmem = pl.BlockSpec(memory_space=pltpu.VMEM)
    anywhere = pl.BlockSpec(memory_space=pl.ANY)
    shapes = weight_shapes()
    operands = [features, order, norm, *shards]
    in_specs = [anywhere, in_vmem, in_vmem] + [in_vmem if plan.inside else anywhere] * 5
    results = [
        ((rows, C_IN), bf16, anywhere),
        ((rows, C_MID), bf16, anywhere),
        (shapes[0], bf16, anywhere),
        ((views, C_IN), f32, anywhere),
        ((2, norm_width()), f32, in_vmem),
        ((8, LANES), f32, in_vmem),
    ]
    for which, shard in enumerate(shards):
        if plan.inside:
            results.append((shard.shape, f32, in_vmem))
        else:
            results.append((shapes[which], bf16, anywhere))
    dma = pltpu.SemaphoreType.DMA

    def sum_room(width):
        return SumRoom(
            pltpu.VMEM((plan.dp, 2, width), f32),
            pltpu.VMEM((plan.fsdp, 2, width), f32),
            dma((plan.dp,)),
            dma((plan.dp,)),
            dma((plan.fsdp,)),
            dma((plan.fsdp,)),
        )

    def matrix_room():
        size = plan.embed_rows
        return MatrixRoom(
            pltpu.VMEM((plan.dp, size, P_OUT), f32),
            pltpu.VMEM((plan.dp, size, P_OUT), f32),
            pltpu.VMEM((plan.fsdp, size, P_OUT), f32),
            pltpu.VMEM((plan.dp, size, P_OUT), f32),
            dma((plan.dp,)),
            dma((plan.dp,)),
            dma((plan.fsdp,)),
            dma((plan.fsdp,)),
            dma((plan.dp,)),
            dma((plan.dp,)),
        )

    scratch = Mem(
        w=[pltpu.VMEM(shape, bf16) for shape in shapes],
        r3=pltpu.VMEM(shapes[2], bf16),
        r4=pltpu.VMEM(shapes[3], bf16),
        r5=pltpu.VMEM(shapes[4], bf16),
        stage=pltpu.VMEM((max(3 * BLOCKS * plan.chunk, 9 * C_MID), C_MID), bf16),
        stage_sem=dma((2, 3, BLOCKS)),
        column_sem=dma((BLOCKS + 3,)),
        h1=pltpu.VMEM((rows, C_MID), bf16),
        d1=pltpu.VMEM((rows, C_MID), bf16),
        h2=pltpu.VMEM((rows, C_MID), bf16),
        d2=pltpu.VMEM((rows, C_MID), bf16),
        a2=pltpu.VMEM((rows, C_MID), bf16),
        h3=pltpu.VMEM((BLOCKS * rows, C_MID), bf16),
        pad1=pltpu.VMEM((SIDE + 2, (SIDE + 2) * views, C_MID), bf16),
        pad2=pltpu.VMEM((SIDE + 2, (SIDE + 2) * views, C_MID), bf16),
        pool=pltpu.VMEM((views, C_IN), f32),
        pool_slope=pltpu.VMEM((views, C_IN), f32),
        pool_bend=pltpu.VMEM((views, C_IN), f32),
        pooled=pltpu.VMEM((views, C_IN), bf16),
        proj_act=pltpu.VMEM((views, P_HID), bf16),
        proj_slope=pltpu.VMEM((views, P_HID), f32),
        proj_hidden=pltpu.VMEM((views, P_HID), f32),
        coef=pltpu.VMEM((8, C_IN), f32),
        stats=pltpu.VMEM((2, norm_width()), f32),
        norm=pltpu.VMEM((2, norm_width()), f32),
        norm_tiles=pltpu.VMEM((plan.dp, plan.fsdp, 2, LANES), f32),
        norm_s0=dma((plan.dp,)),
        norm_r0=dma((plan.dp,)),
        norm_s1=dma((plan.fsdp,)),
        norm_r1=dma((plan.fsdp,)),
        bulk_send=dma((300,)),
        bulk_recv=dma((300,)),
        mats=[matrix_room(), matrix_room()],
        sums=[
            sum_room(width)
            for width in (C_MID, C_MID, C_IN, P_HID, LANES)
        ],
        squares=pltpu.VMEM((1, LANES), f32),
    )
    values = pl.pallas_call(
        lambda *refs: kernel(plan, *refs),
        out_shape=[jax.ShapeDtypeStruct(shape, kind) for shape, kind, _ in results],
        in_specs=in_specs,
        out_specs=[spec for _, _, spec in results],
        scratch_shapes=[scratch],
        compiler_params=pltpu.CompilerParams(
            collective_id=1, has_side_effects=True, vmem_limit_bytes=63 * 2**20
        ),
        name="train_step",
    )(*operands)
    return Outs(*values[:6], values[6:])


def norm_width():
    return 2 * C_MID + C_IN + P_HID


def adam_update(weight, moment_one, moment_two, gradient, step_rate, weight_decay):
    first_new = beta_first * moment_one + (1.0 - beta_first) * gradient
    second_new = beta_second * moment_two + (1.0 - beta_second) * gradient * gradient
    first_hat = first_new / (1.0 - beta_first**STEP)
    second_hat = second_new / (1.0 - beta_second**STEP)
    weight_new = weight - step_rate * (
        first_hat / (jnp.sqrt(second_hat) + adam_epsilon) + weight_decay * weight
    )
    return (weight_new, first_new, second_new)


def gather_full(weight):
    outer = lax.all_gather(weight.astype(bf16), FSDP, axis=0, tiled=True)
    return lax.all_gather(outer, DP, axis=1, tiled=True)


def scatter_full(gradient):
    inner = lax.psum_scatter(gradient.astype(f32), DP, scatter_dimension=1, tiled=True)
    return lax.psum_scatter(inner, FSDP, scatter_dimension=0, tiled=True)


def body(features, view_order, *state):
    masters, firsts, seconds = state[:6], state[6:12], state[12:18]
    dp_size, fsdp_size = lax.axis_size(DP), lax.axis_size(FSDP)
    views = features.shape[0]
    inside = dp_size == 4 and fsdp_size == 8
    plan = Plan(dp_size, fsdp_size, views, inside)
    image_total = views * plan.devices // 2
    pixels = jnp.swapaxes(features, 0, 1).reshape(-1, C_IN)
    norm_params = masters[5]
    shapes = weight_shapes()
    if inside:
        shards = list(masters[:4]) + [masters[4].T]
        norm = norm_params
    else:
        full = [gather_full(weight) for weight in masters[:5]]
        shards = [
            full[0].reshape(shapes[0]),
            full[1],
            full[2].reshape(C_MID, BLOCKS, C_MID).swapaxes(0, 1).reshape(shapes[2]),
            full[3].reshape(shapes[3]),
            full[4].reshape(4, 2, P_OUT, P_OUT).swapaxes(2, 3),
        ]
        norm = lax.all_gather(norm_params.astype(bf16), (DP, FSDP), axis=1, tiled=True).astype(f32)
    got = run_kernel(plan, pixels, view_order, shards, norm)
    grads = list(got.grads)
    squares = jnp.sum(got.scalars[1])
    if inside:
        owned = grads[:4] + [grads[4].T]
    else:
        whole_grads = [
            grads[0].reshape(C_IN, C_MID),
            grads[1],
            grads[2].reshape(BLOCKS, C_MID, C_MID).swapaxes(0, 1).reshape(C_MID, C_IN),
            grads[3].reshape(C_IN, P_HID),
            grads[4].swapaxes(2, 3).reshape(P_HID, P_OUT),
        ]
        owned = [scatter_full(gradient) for gradient in whole_grads]
        squares = squares + lax.psum(sum(jnp.sum(grad * grad) for grad in owned), (DP, FSDP))
    width = norm_params.shape[1]
    owner = lax.axis_index((DP, FSDP))
    owned.append(lax.dynamic_slice_in_dim(got.norm_grad, owner * width, width, 1))
    grad_norm = jnp.sqrt(squares)
    factor = clip_level / jnp.maximum(grad_norm, clip_level)

    summed_grad = got.slope.reshape(PIX, views, C_IN).astype(f32) * got.pool_grad[None]
    back = lax.dot_general(
        got.one_low, got.low_one.reshape(C_IN, C_MID), (((1,), (1,)), ((), ())), preferred_element_type=f32
    )
    input_grad = jnp.swapaxes(summed_grad + back.reshape(PIX, views, C_IN), 0, 1)

    step_rates = (
        C_IN ** (-0.5),
        (9 * C_MID) ** (-0.5),
        C_MID ** (-0.5),
        C_IN ** (-0.5),
        P_HID ** (-0.5),
        norm_rate,
    )
    decays = (decay_rate, decay_rate, decay_rate, decay_rate, decay_rate, 0.0)
    updates = [
        adam_update(masters[i], firsts[i], seconds[i], owned[i] * factor, step_rates[i], decays[i]) for i in range(6)
    ]
    return (
        jnp.sum(got.scalars[0]) / image_total,
        input_grad,
        grad_norm,
        *[update[0] for update in updates],
        *[update[1] for update in updates],
        *[update[2] for update in updates],
    )


def solution(mesh):
    views = P((DP, FSDP), None, None)
    split = P(FSDP, DP)
    norm = P(None, (DP, FSDP))
    params = (split,) * 5 + (norm,)
    return jax.shard_map(
        body,
        mesh=mesh,
        in_specs=(views, P((DP, FSDP), None)) + params * 3,
        out_specs=(P(), views, P()) + params * 3,
        check_vma=False,
    )
```

time: 2060 us -> 351 us (0.17)
  waiting for transfers between devices: 670 us -> 0 us
  blocking collectives: 561 us -> 0 us
  local copies, waits for them, and re-layouts: 397 us -> 0.12 us
  Pallas kernels: 0 us -> 325 us
  other arithmetic: 246 us -> 6.95 us
  matrix products: 152 us -> 14.7 us
    reduce_scatter x10 -> x0, waiting for transfers between devices: 455 us -> none  [the longest x1 81.6 us: reduce_inner(): lax.psum_scatter(grad_two, 'dp', scatter_dimension=1, tiled=True)]
    psum x11 -> x0, blocking collectives: 437 us -> none  [the longest x4 160 us: norm_forward(): lax.psum((jnp.sum(hidden, axis=0), jnp.sum(hidden * hidden, axis=0)), ('d...]
    pallas_call x0 -> x1, Pallas kernels: none -> 325 us  [run_kernel(): pl.pallas_call(lambda *refs: kernel(plan, *refs), out_shape=[jax.ShapeDty...]
    psum x2 -> x0, waiting for transfers between devices: 205 us -> none  [the longest x1 123 us: body(): view_sums, view_outer = lax.psum((view_sums, view_outer), ('dp', 'fsdp'))]
    slice x13 -> x0, local copies, waits for them, and re-layouts: 146 us -> none  [the longest x9 146 us: fold_columns(): picture[:, :, :, 3 * vertical + lateral, :]]
    dot_general x24 -> x1, matrix products: 150 us -> 14.7 us  [body(): lax.dot_general(got.one_low, got.low_one.reshape(C_IN, C_MID), (((1,), (1...]
    all_gather x6 -> x0, blocking collectives: 124 us -> none  [the longest x1 35.7 us: gather_weights(): lax.all_gather(weight_one, 'fsdp', axis=0, tiled=True)]
    reshape x7 -> x0, local copies, waits for them, and re-layouts: 117 us -> none  [the longest x1 52.2 us: fold_columns(): picture = columns_grad.reshape(view_count, SIDE, SIDE, 9, C_MID)]
  transfers between devices with their start and end apart: 18 -> 0, of which waited for: 11 -> 0; matrix products, arithmetic and copies ran while one was open for 34% -> 0% of each run, Pallas kernels for 0% -> 0%
where the time goes in v1:
time: 351 us
  Pallas kernels  325 us (93%)
  matrix products  14.7 us (4%)
  other arithmetic  6.95 us (2%)
  between operations  4.56 us (1%)
    pallas_call x1, Pallas kernels, run_kernel(): pl.pallas_call(lambda *refs: kernel(plan, *refs), out_shape=[jax.ShapeDty...  325 us
    dot_general x1, matrix products, body(): lax.dot_general(got.one_low, got.low_one.reshape(C_IN, C_MID), (((1,), (1...  14.7 us

profile of v1, /device:TPU:0, one launch (start us, length us, event | category | flops | bytes accessed | tf_op | source)
XLA Modules:
  0.0 351.2 jit_solution(910125938949868387)
XLA Ops:
  0.7 0.0 copy-start.20
  0.7 0.0 copy-start.21
  0.7 0.0 copy-start.22
  0.7 324.8 %train_step.1 = (bf16[2352,2048]{1,0:T(8,128)(2,1)}, bf16[2352,512]{1,0:T(8,128)(2,1)}, bf16[4,2,256,512]{3,2,1,0:T(8,128)(2,1)}, f32[48,2048]{1,0:T(8,128)}, f3...) custom-call(bf16[2352,2048]{1,0:T(8,128)(2,1)} %bitcast.21, ...), custom_call_target="tpu_custom_call" | custom-call | tf_op jit(solution)/shard_map/train_step/pallas_call | solution.py:1370
  325.5 1.4 slice_reduce_fusion
  327.6 0.0 copy-done.20
  327.7 0.0 copy-done.21
  327.7 0.0 copy-done.22
  327.7 1.3 multiply_subtract_fusion.5
  329.0 0.0 copy-start.1
  329.0 0.0 copy-start.7
  329.0 0.0 copy-start.8
  329.0 0.0 copy-start.9
  329.0 0.0 copy-start.2
  329.0 0.0 copy-start.10
  329.0 0.0 copy-start.11
  329.1 0.0 copy-start.3
  329.1 0.0 copy-start.12
  329.1 0.0 copy-start.13
  329.1 0.0 copy-start.16
  329.1 0.0 copy-start.17
  329.1 0.0 copy-start.18
  329.1 14.7 %fusion.1 = f32[48,49,2048]{2,0,1:T(8,128)} fusion(bf16[49,48,2048]{2,1,0:T(8,128)(2,1)} %bitcast.23, f32[48,2048]{1,0:T(8,128)} %get-tuple-element.34, bf16[49,48,512]{2,1,0:T(8,128)(2,1)} %bitcast.24, bf16[2048,512,1]{1,0,2:T(8,128)(2,1)} %bitcast.25), kind=kOutput, calls=%fused_computation.2 | convolution fusion | flops 4946952192 | bytes 33800192 | tf_op jit(solution)/shard_map/dot_general | solution.py:1454
  343.9 0.0 copy-done
  343.9 1.1 multiply_subtract_fusion
  345.0 0.0 copy-done.7
  345.0 1.0 multiply_subtract_fusion.1
  346.0 0.8 multiply_subtract_fusion.2
  346.9 0.8 multiply_subtract_fusion.3
  347.7 0.0 copy-done.16
  347.7 0.0 copy-done.18
  347.7 0.6 multiply_subtract_fusion.4
  (23 shorter events, 0.0 us)
Async XLA Ops:
  0.7 327.0 %copy-start.20 = (f32[2,128]{1,0:T(2,128)S(1)}, f32[2,128]{1,0:T(2,128)}, u32[]{:S(2)}) copy-start(f32[2,128]{1,0:T(2,128)} %refs_2_.1) | copy-start | bytes 3076
  0.7 327.0 %copy-start.21 = (f32[2,128]{1,0:T(2,128)S(1)}, f32[2,128]{1,0:T(2,128)}, u32[]{:S(2)}) copy-start(f32[2,128]{1,0:T(2,128)} %param.33) | copy-start | bytes 3076
  0.7 327.0 %copy-start.22 = (f32[2,128]{1,0:T(2,128)S(1)}, f32[2,128]{1,0:T(2,128)}, u32[]{:S(2)}) copy-start(f32[2,128]{1,0:T(2,128)} %param.39) | copy-start | bytes 3076
  328.9 14.9 %copy-start = (f32[576,128]{1,0:T(8,128)S(1)}, f32[576,128]{1,0:T(8,128)}, u32[]{:S(2)}) copy-start(f32[576,128]{1,0:T(8,128)} %refs_4_.1) | copy-start | bytes 884740
  328.9 14.9 %copy-start.4 = (f32[576,128]{1,0:T(8,128)S(1)}, f32[576,128]{1,0:T(8,128)}, u32[]{:S(2)}) copy-start(f32[576,128]{1,0:T(8,128)} %param.29) | copy-start | bytes 884740
  329.0 14.9 %copy-start.5 = (f32[576,128]{1,0:T(8,128)S(1)}, f32[576,128]{1,0:T(8,128)}, u32[]{:S(2)}) copy-start(f32[576,128]{1,0:T(8,128)} %param.35) | copy-start | bytes 884740
  329.0 15.0 %copy-start.6 = (f32[576,128]{1,0:T(8,128)S(1)}, f32[576,128]{1,0:T(8,128)}, u32[]{:S(2)}) copy-start(f32[576,128]{1,0:T(8,128)} %get-tuple-element.38) | copy-start | bytes 884740
  329.0 16.0 %copy-start.1 = (f32[256,256]{1,0:T(8,128)S(1)}, f32[256,256]{1,0:T(8,128)}, u32[]{:S(2)}) copy-start(f32[256,256]{1,0:T(8,128)} %refs_6_.1) | copy-start | bytes 786436
  329.0 16.0 %copy-start.7 = (f32[256,256]{1,0:T(8,128)S(1)}, f32[256,256]{1,0:T(8,128)}, u32[]{:S(2)}) copy-start(f32[256,256]{1,0:T(8,128)} %param.31) | copy-start | bytes 786436
  329.0 16.0 %copy-start.8 = (f32[256,256]{1,0:T(8,128)S(1)}, f32[256,256]{1,0:T(8,128)}, u32[]{:S(2)}) copy-start(f32[256,256]{1,0:T(8,128)} %param.37) | copy-start | bytes 786436
  329.0 16.0 %copy-start.9 = (f32[256,256]{1,0:T(8,128)S(1)}, f32[256,256]{1,0:T(8,128)}, u32[]{:S(2)}) copy-start(f32[256,256]{1,0:T(8,128)} %get-tuple-element.40) | copy-start | bytes 786436
  329.0 17.0 %copy-start.2 = (f32[64,512]{1,0:T(8,128)S(1)}, f32[64,512]{1,0:T(8,128)}, u32[]{:S(2)}) copy-start(f32[64,512]{1,0:T(8,128)} %refs_5_.1) | copy-start | bytes 393220
  329.0 17.0 %copy-start.10 = (f32[64,512]{1,0:T(8,128)S(1)}, f32[64,512]{1,0:T(8,128)}, u32[]{:S(2)}) copy-start(f32[64,512]{1,0:T(8,128)} %param.30) | copy-start | bytes 393220
  329.0 17.0 %copy-start.11 = (f32[64,512]{1,0:T(8,128)S(1)}, f32[64,512]{1,0:T(8,128)}, u32[]{:S(2)}) copy-start(f32[64,512]{1,0:T(8,128)} %param.36) | copy-start | bytes 393220
  329.0 17.0 %copy-start.15 = (f32[64,512]{1,0:T(8,128)S(1)}, f32[64,512]{1,0:T(8,128)}, u32[]{:S(2)}) copy-start(f32[64,512]{1,0:T(8,128)} %get-tuple-element.39) | copy-start | bytes 393220
  329.1 17.8 %copy-start.3 = (f32[256,128]{1,0:T(8,128)S(1)}, f32[256,128]{1,0:T(8,128)}, u32[]{:S(2)}) copy-start(f32[256,128]{1,0:T(8,128)} %refs_3_.1) | copy-start | bytes 393220
  329.1 17.8 %copy-start.12 = (f32[256,128]{1,0:T(8,128)S(1)}, f32[256,128]{1,0:T(8,128)}, u32[]{:S(2)}) copy-start(f32[256,128]{1,0:T(8,128)} %param.28) | copy-start | bytes 393220
  329.1 17.8 %copy-start.13 = (f32[256,128]{1,0:T(8,128)S(1)}, f32[256,128]{1,0:T(8,128)}, u32[]{:S(2)}) copy-start(f32[256,128]{1,0:T(8,128)} %param.34) | copy-start | bytes 393220
  329.1 17.8 %copy-start.14 = (f32[256,128]{1,0:T(8,128)S(1)}, f32[256,128]{1,0:T(8,128)}, u32[]{:S(2)}) copy-start(f32[256,128]{1,0:T(8,128)} %get-tuple-element.37) | copy-start | bytes 393220
  329.1 18.6 %copy-start.16 = (f32[128,32]{0,1:T(8,128)S(1)}, f32[128,32]{0,1:T(8,128)}, u32[]{:S(2)}) copy-start(f32[128,32]{0,1:T(8,128)} %param.26) | copy-start | bytes 49156
  329.1 18.6 %copy-start.17 = (f32[128,32]{0,1:T(8,128)S(1)}, f32[128,32]{0,1:T(8,128)}, u32[]{:S(2)}) copy-start(f32[128,32]{0,1:T(8,128)} %param.32) | copy-start | bytes 49156
  329.1 18.5 %copy-start.18 = (f32[128,32]{0,1:T(8,128)S(1)}, f32[128,32]{0,1:T(8,128)}, u32[]{:S(2)}) copy-start(f32[128,32]{0,1:T(8,128)} %param.38) | copy-start | bytes 49156
  329.1 18.5 %copy-start.19 = (f32[32,128]{1,0:T(8,128)S(1)}, f32[32,128]{1,0:T(8,128)}, u32[]{:S(2)}) copy-start(f32[32,128]{1,0:T(8,128)} %get-tuple-element.41) | copy-start | bytes 49156
